TPU v7x, 32 devices: a whole 2x2x4 slice. The times are simulated.
32 devices in a mesh: gx: 4 (over x, core), gy: 2 (over y), gz: 4 (over z).
Axes of the slice: x: 2, y: 2, z: 4, core: 2. Of those that a mesh axis runs over, the one named last changes fastest.
Arguments:
- features: float32 [128, 64, 512], P(('gx', 'gy', 'gz')), may hold values from -6 to 6
- preact: float32 [128, 64, 512], P(('gx', 'gy', 'gz')), may hold values from -10 to 10
- cotangent: float32 [128, 64, 512], P(('gx', 'gy', 'gz')), may hold values from -6 to 6
- kernel: float32 [27, 64, 64], replicated, may hold values from -0.15625 to 0.15625
- active: int32 [128, 512], P(('gx', 'gy', 'gz')), may hold values from 0 to 1, as said below
- owner_dir: int32 [128, 27], P(('gx', 'gy', 'gz')), may hold values from 0 to 27, as said below
- owner_slot: int32 [128, 27], P(('gx', 'gy', 'gz')), may hold values from 0 to 3, as said below
- send_list: int32 [96], P(('gx', 'gy', 'gz')), may hold values from 0 to 4, as said below
Outputs:
- input_grad: float32 [128, 64, 512], P(('gx', 'gy', 'gz'))
- kernel_grad: float32 [27, 64, 64], replicated
- bias_grad: float32 [64], replicated
Inputs may be any that keep to these rules, and one draw needn't show every extreme that they name: `owner_dir`: 27 where the neighbouring block is empty or the stored entry is unused; 13 for a block of the same partition; else the offset of the owner's grid position, 9 (dx + 1) + 3 (dy + 1) + (dz + 1), with dx, dy, dz each -1, 0 or 1. A named partition always exists and lists the block in its send list. `owner_slot`: own stored index where owner_dir is 13, position in the owner's send list where owner_dir names another partition, 0 where it is 27. `send_list`: each partition's 3 entries hold, increasing, the distinct stored indices of its occupied blocks in the partition's outer layer of blocks (on faces, edges or corners), each of which touches another partition, then 4 for unused entries; some partition fills all 3. 1 for active voxels of an occupied stored block, 0 elsewhere; unused stored entries are 0 throughout; some partition has all 4 entries occupied.
All inputs are finite; a program needn't handle non-finite values.
Results may differ from a plain program's by a relative error of at most 0.0001.
Values sent between devices are 32-bit elements; how exact they have to be, the bound alone decides.
A program may use at most 64 MiB of HBM per device.

v0:
```python
import jax
import jax.numpy as jnp
from jax import lax
from jax.sharding import PartitionSpec as P

BS = 8


def padded_2(cells, sides, width):
    for axis, dim in sides:
        count = lax.axis_size(axis)
        ends = count - 1
        head = lax.slice_in_dim(cells, 0, width, axis=dim)
        tail = lax.slice_in_dim(cells, cells.shape[dim] - width, cells.shape[dim], axis=dim)
        cells = jnp.concatenate(
            [
                lax.ppermute(tail, axis, [(i, (i + 1) % count) for i in range(ends)]),
                cells,
                lax.ppermute(head, axis, [((i + 1) % count, i) for i in range(ends)]),
            ],
            axis=dim,
        )
    return cells


def silu_slope(preact):
    sigmoid_value = jax.nn.sigmoid(preact)
    return sigmoid_value * (1.0 + preact * (1.0 - sigmoid_value))


def shifted_stack(padded, direction, extent):
    windows = []
    for offset_x in (-1, 0, 1):
        for offset_y in (-1, 0, 1):
            for offset_z in (-1, 0, 1):
                begin_x = 1 + direction * offset_x
                begin_y = 1 + direction * offset_y
                begin_z = 1 + direction * offset_z
                window = padded[
                    :,
                    begin_x : begin_x + extent,
                    begin_y : begin_y + extent,
                    begin_z : begin_z + extent,
                ]
                windows.append(window.reshape(padded.shape[0], extent**3))
    return jnp.stack(windows)


def slice_length(heading, extent):
    length = 1
    for move in heading:
        length = length * (extent if move == 0 else 1)
    return length


def cut_slice(cubes, heading, extent):
    ranges = [
        slice(extent - 1, extent) if move == 1 else slice(0, 1) if move == -1 else slice(0, extent)
        for move in heading
    ]
    portion = cubes[:, :, ranges[0], ranges[1], ranges[2]]
    return portion.reshape(cubes.shape[0], cubes.shape[1], -1)


def remote_piece(sheet_row, owner_offset, block_offset, extent):
    sheet_side = tuple((-move for move in owner_offset))
    block_side = tuple((-move for move in block_offset))
    lengths = tuple((extent if move == 0 else 1 for move in sheet_side))
    shaped = sheet_row.reshape((sheet_row.shape[0],) + lengths)
    ranges = []
    for sheet_move, block_move in zip(sheet_side, block_side):
        if sheet_move == 0 and block_move == 1:
            ranges.append(slice(extent - 1, extent))
        elif sheet_move == 0 and block_move == -1:
            ranges.append(slice(0, 1))
        else:
            ranges.append(slice(None))
    return shaped[:, ranges[0], ranges[1], ranges[2]]


def options_along(move):
    return (0,) if move == 0 else (0, move)


def gather_cube(own_cubes, sheets, targets, slots, extent, listed):
    anchor = jnp.zeros((), jnp.int32)
    blocks, width = (own_cubes.shape[0], own_cubes.shape[1])
    remote_row = jnp.clip(slots, 0, listed - 1)
    own_row = jnp.clip(slots, 0, blocks - 1)
    layers = []
    for place_x in range(3):
        strips = []
        for place_y in range(3):
            pieces = []
            for place_z in range(3):
                places = (place_x, place_y, place_z)
                block_offset = (place_x - 1, place_y - 1, place_z - 1)
                index = place_x * 9 + place_y * 3 + place_z
                begins = [anchor + (extent - 1 if where_at == 0 else 0) for where_at in places]
                lengths = [extent if where_at == 1 else 1 for where_at in places]
                code_here = targets[index]
                own_part = lax.dynamic_slice(
                    own_cubes, [own_row[index], anchor] + begins, [1, width] + lengths
                )[0]
                piece = jnp.where(code_here == 13, own_part, jnp.zeros_like(own_part))
                for move_x in options_along(block_offset[0]):
                    for move_y in options_along(block_offset[1]):
                        for move_z in options_along(block_offset[2]):
                            owner_offset = (move_x, move_y, move_z)
                            if owner_offset == (0, 0, 0):
                                continue
                            code = 9 * (move_x + 1) + 3 * (move_y + 1) + (move_z + 1)
                            sheet_row = lax.dynamic_index_in_dim(
                                sheets[owner_offset], remote_row[index], 0, keepdims=False
                            )
                            piece = jnp.where(
                                code_here == code,
                                remote_piece(sheet_row, owner_offset, block_offset, extent),
                                piece,
                            )
                pieces.append(piece)
            strips.append(jnp.concatenate(pieces, axis=3))
        layers.append(jnp.concatenate(strips, axis=2))
    return jnp.concatenate(layers, axis=1)


def shards(features, preact, cotangent, kernel, active, owner_dir, owner_slot, send_list):
    blocks, channels, volume = features.shape
    extent = BS
    listed = send_list.shape[0]
    voxel_mask = active.astype(jnp.float32)[:, None, :]
    gradient = cotangent * silu_slope(preact) * voxel_mask
    masked_input = features * voxel_mask
    keep_mask = (send_list < blocks).astype(jnp.float32)[:, None, None]
    picked = jnp.minimum(send_list, blocks - 1)
    grad_pack = gradient[picked] * keep_mask
    payload = jnp.concatenate([grad_pack, masked_input[picked] * keep_mask], axis=1)
    own_all = jnp.concatenate([gradient, masked_input], axis=1)
    width_all = payload.shape[1]
    cubes = payload.reshape(listed, width_all, extent, extent, extent)
    own_cubes = own_all.reshape(blocks, width_all, extent, extent, extent)
    headings = [
        (move_x, move_y, move_z)
        for move_x in (-1, 0, 1)
        for move_y in (-1, 0, 1)
        for move_z in (-1, 0, 1)
    ]
    centre = (0, 0, 0)
    sheets = {}
    layers = []
    for heading in headings:
        if heading == centre:
            layers.append(jnp.zeros((listed, width_all, extent * extent), jnp.float32))
        else:
            portion = cut_slice(cubes, heading, extent)
            layers.append(
                jnp.pad(portion, ((0, 0), (0, 0), (0, extent * extent - portion.shape[2])))
            )
    packed = jnp.stack(layers).reshape((3, 3, 3, listed, width_all, extent * extent))
    grown = padded_2(packed, (("gx", 0), ("gy", 1), ("gz", 2)), 1)
    for offset in headings:
        if offset != centre:
            backward = tuple((-move for move in offset))
            sheet = grown[2 + 2 * offset[0], 2 + 2 * offset[1], 2 + 2 * offset[2]]
            sheets[offset] = sheet[:, :, : slice_length(backward, extent)]

    def visit_block(running, inputs):
        kernel_partial, bias_partial = running
        targets, slots, own_grad, own_input, own_mask = inputs
        whole_cube = gather_cube(own_cubes, sheets, targets, slots, extent, listed)
        grad_windows = shifted_stack(whole_cube[:channels], -1, extent)
        block_result = (
            jnp.einsum("kio,kov->iv", kernel, grad_windows, precision=lax.Precision.HIGHEST)
            * own_mask
        )
        input_windows = shifted_stack(whole_cube[channels:], 1, extent)
        kernel_partial = kernel_partial + jnp.einsum(
            "kiv,ov->kio", input_windows, own_grad, precision=lax.Precision.HIGHEST
        )
        bias_partial = bias_partial + jnp.sum(own_grad, axis=1)
        return ((kernel_partial, bias_partial), block_result)

    initial = (
        jnp.zeros((27, channels, channels), jnp.float32),
        jnp.zeros((channels,), jnp.float32),
    )
    (kernel_partial, bias_partial), input_grad = lax.scan(
        visit_block, initial, (owner_dir, owner_slot, gradient, masked_input, voxel_mask)
    )
    kernel_total, bias_total = lax.psum((kernel_partial, bias_partial), ("gx", "gy", "gz"))
    scaling = (volume * blocks * lax.axis_size(("gx", "gy", "gz"))) ** (-0.5)
    return (input_grad, kernel_total * scaling, bias_total * scaling)


def solution(mesh):
    placed = (
        P(("gx", "gy", "gz"), None, None),
        P(("gx", "gy", "gz"), None, None),
        P(("gx", "gy", "gz"), None, None),
        P(),
        P(("gx", "gy", "gz"), None),
        P(("gx", "gy", "gz"), None),
        P(("gx", "gy", "gz"), None),
        P(("gx", "gy", "gz")),
    )
    return jax.shard_map(
        shards,
        mesh=mesh,
        in_specs=placed,
        out_specs=(P(("gx", "gy", "gz"), None, None), P(), P()),
        check_vma=False,
    )
```

profile of v0, /device:TPU:0, one launch (start us, length us, event | category | flops | bytes accessed | tf_op | source)
XLA Modules:
  0.0 1857.5 jit_solution(4337713397638752874)
XLA Ops:
  10.6 2.4 copy.564
  13.0 2.3 copy.566
  25.3 3.1 collective-permute-start
  30.7 5.0 collective-permute-start.2
  37.0 23.1 %collective-permute-done.2 = f32[5,1,3,3,128,64]{4,5,3,2,1,0:T(8,128)S(1)} collective-permute-done((f32[5,1,3,3,128,64]{4,5,3,2,1,0:T(8,128)S(1)}, f32[5,1,3,3,128,64]{4,5,3,2,1,0:T(8,128)S(1)}, u32[]{:S(2)}, u32[]{:S(2)}) %collective-permute-start.2) | collective-permute-done | bytes 1474592 | tf_op jit(solution)/shard_map/ppermute | solution.py:17
  60.1 4.8 collective-permute-done.3
  64.9 2.7 pad_maximum_fusion.6
  68.9 6.0 collective-permute-start.4
  82.3 37.0 %collective-permute-done.5 = f32[5,5,1,3,128,64]{4,5,3,2,1,0:T(8,128)} collective-permute-done((f32[5,5,1,3,128,64]{4,5,3,2,1,0:T(8,128)}, f32[5,5,1,3,128,64]{4,5,3,2,1,0:T(8,128)}, u32[]{:S(2)}, u32[]{:S(2)}) %collective-permute-start.5) | collective-permute-done | bytes 2457632 | tf_op jit(solution)/shard_map/ppermute | solution.py:19
  131.1 1583.7 %while.15 = (s32[]{:T(128)}, f32[27,64,64]{2,1,0:T(8,128)}, f32[64]{0:T(128)}, f32[4,64,512]{2,1,0:T(8,128)}, s32[4,27]{1,0:T(4,128)}, /*index=5*/s32[4,27]{1,0:...) while((s32[]{:T(128)}, f32[27,64,64]{2,1,0:T(8,128)}, ...), condition=%wide.region_2.3_spmd.clone, body=%wide.region_0.2_spmd.clone.sunk | while | flops 1361610112 | bytes 96052456 | solution.py:187
  370.3 2.5 fusion.234
  479.4 5.2 convolution_add_fusion.2
  523.4 3.1 fusion.240
  766.4 2.5 fusion.234
  875.5 5.2 convolution_add_fusion.2
  919.4 3.1 fusion.240
  1162.5 2.5 fusion.234
  1271.6 5.2 convolution_add_fusion.2
  1315.6 3.1 fusion.240
  1558.6 2.5 fusion.234
  1667.7 5.2 convolution_add_fusion.2
  1711.7 3.1 fusion.240
  1714.9 44.6 %psum.15 = f32[64]{0:T(128)S(1)} all-reduce(f32[64]{0:T(128)} %get-tuple-element.189), channel_id=1, replica_groups=mesh['gx'=4,'gy'=2,'gz'=4] {'gx','gy','gz'}, use_global_device_ids=true, to_apply=%region_4.5 | all-reduce | flops 64 | bytes 512 | tf_op jit(solution)/shard_map/psum | solution.py:190
  1760.0 88.5 %all-reduce.22.cloned.1.call-done = f32[27,64,64]{2,1,0:T(8,128)} async-done(((f32[27,64,64]{2,1,0:T(8,128)}), f32[27,64,64]{2,1,0:T(8,128)}) %all-reduce.22.cloned.1.call-update) | async-done | bytes 442384 | tf_op jit(solution)/shard_map/psum | solution.py:190
  (1305 shorter events, 874.6 us)
Async XLA Ops:
  7.2 1841.3 %all-reduce.22.cloned.1.call-start = ((), (), s32[]{:S(2)}) async-start(), calls=%async_computation | async-start | bytes 1769472 | tf_op jit(solution)/shard_map/psum | solution.py:190
  22.7 5.7 collective-permute-start.1
  25.3 5.1 collective-permute-start
  30.7 29.4 %collective-permute-start.2 = (f32[5,1,3,3,128,64]{4,5,3,2,1,0:T(8,128)S(1)}, f32[5,1,3,3,128,64]{4,5,3,2,1,0:T(8,128)S(1)}, u32[]{:S(2)}, u32[]{:S(2)}) collective-permute-start(f32[5,1,3,3,128,64]{4,5,3,2,1,0:T(8,128)S(1)} %get-tuple-element.752), channel_id=1, source_target_pairs={{0,4},{1,5},{2,6},{3,7},{8,12},{9,13},{10,14},{11,15},{16,20},{17,... | collective-permute-start | bytes 4423688 | tf_op jit(solution)/shard_map/ppermute | solution.py:17
  35.7 29.2 %collective-permute-start.3 = (f32[5,1,3,3,128,64]{4,5,3,2,1,0:T(8,128)S(1)}, f32[5,1,3,3,128,64]{4,5,3,2,1,0:T(8,128)S(1)}, u32[]{:S(2)}, u32[]{:S(2)}) collective-permute-start(f32[5,1,3,3,128,64]{4,5,3,2,1,0:T(8,128)S(1)} %get-tuple-element.753), channel_id=1, source_target_pairs={{4,0},{5,1},{6,2},{7,3},{12,8},{13,9},{14,10},{15,11},{20,16},{21,... | collective-permute-start | bytes 4423688 | tf_op jit(solution)/shard_map/ppermute | solution.py:19
  67.6 51.6 %collective-permute-start.5 = (f32[5,5,1,3,128,64]{4,5,3,2,1,0:T(8,128)}, f32[5,5,1,3,128,64]{4,5,3,2,1,0:T(8,128)}, u32[]{:S(2)}, u32[]{:S(2)}) collective-permute-start(f32[5,5,1,3,128,64]{4,5,3,2,1,0:T(8,128)} %get-tuple-element.750), channel_id=1, source_target_pairs={{1,0},{2,1},{3,2},{5,4},{6,5},{7,6},{9,8},{10,9},{11,10},{13,12},{... | collective-permute-start | bytes 7372808 | tf_op jit(solution)/shard_map/ppermute | solution.py:19
  68.9 56.3 %collective-permute-start.4 = (f32[5,5,1,3,128,64]{4,5,3,2,1,0:T(8,128)}, f32[5,5,1,3,128,64]{4,5,3,2,1,0:T(8,128)}, u32[]{:S(2)}, u32[]{:S(2)}) collective-permute-start(f32[5,5,1,3,128,64]{4,5,3,2,1,0:T(8,128)} %get-tuple-element.751), channel_id=1, source_target_pairs={{0,1},{1,2},{2,3},{4,5},{5,6},{6,7},{8,9},{9,10},{10,11},{12,13},{... | collective-permute-start | bytes 7372808 | tf_op jit(solution)/shard_map/ppermute | solution.py:17
  131.1 195.9 %copy-start.9 = (f32[3,128,64]{1,2,0:T(8,128)}, f32[3,128,64]{1,2,0:T(8,128)S(1)}, u32[]{:S(2)}) copy-start(f32[3,128,64]{1,2,0:T(8,128)S(1)} %get-tuple-element.1654) | copy-start | bytes 294916 | tf_op jit(solution)/shard_map/while
  131.1 195.9 %copy-start.11 = (f32[3,128,64]{1,2,0:T(8,128)}, f32[3,128,64]{1,2,0:T(8,128)S(1)}, u32[]{:S(2)}) copy-start(f32[3,128,64]{1,2,0:T(8,128)S(1)} %get-tuple-element.1664) | copy-start | bytes 294916 | tf_op jit(solution)/shard_map/while
  131.1 204.1 %copy-start.36 = (f32[3,128,8]{1,2,0:T(8,128)}, f32[3,128,8]{1,2,0:T(8,128)S(1)}, u32[]{:S(2)}) copy-start(f32[3,128,8]{1,2,0:T(8,128)S(1)} %get-tuple-element.1650) | copy-start | bytes 36868 | tf_op jit(solution)/shard_map/while
  131.1 205.5 %copy-start.7 = (f32[3,128,64]{1,2,0:T(8,128)}, f32[3,128,64]{1,2,0:T(8,128)S(1)}, u32[]{:S(2)}) copy-start(f32[3,128,64]{1,2,0:T(8,128)S(1)} %get-tuple-element.1652) | copy-start | bytes 294916 | tf_op jit(solution)/shard_map/while
  526.6 196.6 %copy-start.9 = (f32[3,128,64]{1,2,0:T(8,128)}, f32[3,128,64]{1,2,0:T(8,128)S(1)}, u32[]{:S(2)}) copy-start(f32[3,128,64]{1,2,0:T(8,128)S(1)} %get-tuple-element.1654) | copy-start | bytes 294916 | tf_op jit(solution)/shard_map/while
  526.6 196.6 %copy-start.11 = (f32[3,128,64]{1,2,0:T(8,128)}, f32[3,128,64]{1,2,0:T(8,128)S(1)}, u32[]{:S(2)}) copy-start(f32[3,128,64]{1,2,0:T(8,128)S(1)} %get-tuple-element.1664) | copy-start | bytes 294916 | tf_op jit(solution)/shard_map/while
  526.6 204.8 %copy-start.36 = (f32[3,128,8]{1,2,0:T(8,128)}, f32[3,128,8]{1,2,0:T(8,128)S(1)}, u32[]{:S(2)}) copy-start(f32[3,128,8]{1,2,0:T(8,128)S(1)} %get-tuple-element.1650) | copy-start | bytes 36868 | tf_op jit(solution)/shard_map/while
  526.6 206.2 %copy-start.7 = (f32[3,128,64]{1,2,0:T(8,128)}, f32[3,128,64]{1,2,0:T(8,128)S(1)}, u32[]{:S(2)}) copy-start(f32[3,128,64]{1,2,0:T(8,128)S(1)} %get-tuple-element.1652) | copy-start | bytes 294916 | tf_op jit(solution)/shard_map/while
  922.6 195.1 %copy-start.13 = (f32[3,128,64]{1,2,0:T(8,128)}, f32[3,128,64]{1,2,0:T(8,128)S(1)}, u32[]{:S(2)}) copy-start(f32[3,128,64]{1,2,0:T(8,128)S(1)} %get-tuple-element.1660) | copy-start | bytes 294916 | tf_op jit(solution)/shard_map/while
  922.7 196.6 %copy-start.9 = (f32[3,128,64]{1,2,0:T(8,128)}, f32[3,128,64]{1,2,0:T(8,128)S(1)}, u32[]{:S(2)}) copy-start(f32[3,128,64]{1,2,0:T(8,128)S(1)} %get-tuple-element.1654) | copy-start | bytes 294916 | tf_op jit(solution)/shard_map/while
  922.7 196.6 %copy-start.11 = (f32[3,128,64]{1,2,0:T(8,128)}, f32[3,128,64]{1,2,0:T(8,128)S(1)}, u32[]{:S(2)}) copy-start(f32[3,128,64]{1,2,0:T(8,128)S(1)} %get-tuple-element.1664) | copy-start | bytes 294916 | tf_op jit(solution)/shard_map/while
  922.7 204.8 %copy-start.36 = (f32[3,128,8]{1,2,0:T(8,128)}, f32[3,128,8]{1,2,0:T(8,128)S(1)}, u32[]{:S(2)}) copy-start(f32[3,128,8]{1,2,0:T(8,128)S(1)} %get-tuple-element.1650) | copy-start | bytes 36868 | tf_op jit(solution)/shard_map/while
  922.7 206.2 %copy-start.7 = (f32[3,128,64]{1,2,0:T(8,128)}, f32[3,128,64]{1,2,0:T(8,128)S(1)}, u32[]{:S(2)}) copy-start(f32[3,128,64]{1,2,0:T(8,128)S(1)} %get-tuple-element.1652) | copy-start | bytes 294916 | tf_op jit(solution)/shard_map/while
  1318.8 196.6 %copy-start.9 = (f32[3,128,64]{1,2,0:T(8,128)}, f32[3,128,64]{1,2,0:T(8,128)S(1)}, u32[]{:S(2)}) copy-start(f32[3,128,64]{1,2,0:T(8,128)S(1)} %get-tuple-element.1654) | copy-start | bytes 294916 | tf_op jit(solution)/shard_map/while
  1318.8 196.6 %copy-start.11 = (f32[3,128,64]{1,2,0:T(8,128)}, f32[3,128,64]{1,2,0:T(8,128)S(1)}, u32[]{:S(2)}) copy-start(f32[3,128,64]{1,2,0:T(8,128)S(1)} %get-tuple-element.1664) | copy-start | bytes 294916 | tf_op jit(solution)/shard_map/while
  1318.8 204.8 %copy-start.36 = (f32[3,128,8]{1,2,0:T(8,128)}, f32[3,128,8]{1,2,0:T(8,128)S(1)}, u32[]{:S(2)}) copy-start(f32[3,128,8]{1,2,0:T(8,128)S(1)} %get-tuple-element.1650) | copy-start | bytes 36868 | tf_op jit(solution)/shard_map/while
  1318.8 206.1 %copy-start.7 = (f32[3,128,64]{1,2,0:T(8,128)}, f32[3,128,64]{1,2,0:T(8,128)S(1)}, u32[]{:S(2)}) copy-start(f32[3,128,64]{1,2,0:T(8,128)S(1)} %get-tuple-element.1652) | copy-start | bytes 294916 | tf_op jit(solution)/shard_map/while
  (127 other events, 3415.6 us)
Sparse Core Ops, SparseCore 0:
  1715.0 133.4 all-reduce.21
where the time goes:
time: 1880 us; the launch traced here: 1860 us
  local copies, waits for them, and re-layouts  816 us (43%)
  loops' own time  706 us (38%)
  waiting for transfers between devices  155 us (8%)
  other arithmetic  70.3 us (4%)
  blocking collectives  44.6 us (2%)
  matrix products  33.2 us (2%)
    another operation x1, loops' own time, shards(): lax.scan(visit_block, initial, (owner_dir, owner_slot, gradient, masked_i...  706 us
    reshape x216, local copies, waits for them, and re-layouts, shifted_stack(): return jnp.stack(windows)  273 us
    slice x236, local copies, waits for them, and re-layouts, shifted_stack(): padded[:, begin_x:begin_x + extent, begin_y:begin_y + extent, begin_z:beg...  234 us
    while x496, local copies, waits for them, and re-layouts  215 us
    psum x1, waiting for transfers between devices, shards(): lax.psum((kernel_partial, bias_partial), ('gx', 'gy', 'gz'))  88.5 us
    psum x1, blocking collectives, shards(): lax.psum((kernel_partial, bias_partial), ('gx', 'gy', 'gz'))  44.6 us
    ppermute x3, waiting for transfers between devices, padded_2(): lax.ppermute(head, axis, [((i + 1) % count, i) for i in range(ends)])  41.8 us
    select_n x76, other arithmetic, gather_cube(): jnp.where(code_here == code, remote_piece(sheet_row, owner_offset, block_...  39.5 us
  transfers between devices with their start and end apart: 7, of which 5 were waited for; matrix products, arithmetic and copies ran while one was open for 1% of the time, Pallas kernels for 0%

commit v1 on v0

v1 whole, which is shorter than its diff:
```python
import functools
import itertools

import jax
import jax.numpy as jnp
from jax import lax
from jax.experimental import pallas as pl
from jax.experimental.pallas import tpu as pltpu
from jax.sharding import PartitionSpec as P

BS = 8
LANES = 128
AXES = ("gx", "gy", "gz")
MESH = pl.DeviceIdType.MESH
DEPTH = 3 * BS
CUBE_STEPS = ((BS + 2) * DEPTH, DEPTH, 1)
BLOCK_STEPS = (BS * BS, BS, 1)
HEADINGS = [m for m in itertools.product((-1, 0, 1), repeat=3) if m != (0, 0, 0)]
FACES = [m for m in HEADINGS if sum(map(abs, m)) == 1]
EDGES = [m for m in HEADINGS if sum(map(abs, m)) == 2]
CORNERS = [m for m in HEADINGS if sum(map(abs, m)) == 3]
GROUPS = (FACES, EDGES, CORNERS)


def silu_slope(preact):
    sigmoid_value = jax.nn.sigmoid(preact)
    return sigmoid_value * (1.0 + preact * (1.0 - sigmoid_value))


def place(move):
    group = sum(map(abs, move)) - 1
    return group, GROUPS[group].index(move)


def side_row(move):
    return sum(step * (BS - 1) for step, m in zip(BLOCK_STEPS, move) if m == 1)


def free_axes(move):
    return [axis for axis in range(3) if move[axis] == 0]


def split_lanes(value):
    high = value.astype(jnp.bfloat16).astype(jnp.float32)
    return high + pltpu.roll(value - high, LANES // 2, 1)


def halo_kernel(
    sizes, send_list, preact, cotangent, active, weights, split_grad, split_weights, bias,
    face_in, edge_in, corner_in, grad, picked, face_out, edge_out, corner_out, send_sem, recv_sem,
):
    blocks, channels, volume = preact.shape
    listed = send_list.shape[0]
    here = [lax.axis_index(axis) for axis in AXES]

    def inside(move):
        checks = []
        for axis in range(3):
            if move[axis] == 1:
                checks.append((here[axis] < sizes[axis] - 1).astype(jnp.int32))
            elif move[axis] == -1:
                checks.append((here[axis] > 0).astype(jnp.int32))
        return functools.reduce(lambda a, b: a * b, checks)

    live = {move: inside(move) for move in HEADINGS}
    target = {move: tuple(h + m for h, m in zip(here, move)) for move in HEADINGS}
    barrier = pltpu.get_barrier_semaphore()
    for move in HEADINGS:
        @pl.when(live[move] == 1)
        def _():
            pl.semaphore_signal(barrier, inc=1, device_id=target[move], device_id_type=MESH)

    total = jnp.zeros((1, LANES), jnp.float32)
    for b in range(blocks):
        value = cotangent[b] * silu_slope(preact[b]) * active[pl.ds(b, 1), :].astype(jnp.float32)
        rows = jnp.concatenate([value, jnp.zeros((LANES - channels, volume), jnp.float32)], axis=0).T
        grad[b] = rows
        total = total + jnp.sum(rows, axis=0, keepdims=True)
    bias[...] = jnp.broadcast_to(total, bias.shape)

    for s in range(listed):
        entry = send_list[s]
        keep = (entry < blocks).astype(jnp.float32)
        picked[...] = grad[jnp.minimum(entry, blocks - 1)] * keep
        for f, move in enumerate(FACES):
            first, second = free_axes(move)
            base = side_row(move)
            tiles = [
                picked[pl.ds(base + u * BLOCK_STEPS[first], BS, stride=BLOCK_STEPS[second]), :]
                for u in range(BS)
            ]
            for u in range(BS // 2):
                face_out[f, s, pl.ds(u * BS, BS), :] = tiles[u] + pltpu.roll(
                    tiles[u + BS // 2], LANES // 2, 1
                )
        for f, move in enumerate(EDGES):
            (along,) = free_axes(move)
            edge_out[f, s] = picked[pl.ds(side_row(move), BS, stride=BLOCK_STEPS[along]), :]
        for f, move in enumerate(CORNERS):
            corner_out[f, s] = jnp.broadcast_to(picked[pl.ds(side_row(move), 1), :], (BS, LANES))

    count = functools.reduce(lambda a, b: a + b, [live[move] for move in HEADINGS])
    pl.semaphore_wait(barrier, count)

    sent, landed = (face_out, edge_out, corner_out), (face_in, edge_in, corner_in)

    def copy_of(move):
        group, f = place(move)
        n = HEADINGS.index(move)
        return pltpu.make_async_remote_copy(
            src_ref=sent[group].at[f],
            dst_ref=landed[group].at[f],
            send_sem=send_sem.at[n],
            recv_sem=recv_sem.at[n],
            device_id=target[move],
            device_id_type=MESH,
        )

    for move in FACES + EDGES + CORNERS:
        @pl.when(live[move] == 1)
        def _():
            copy_of(move).start()

    for b in range(blocks):
        split_grad[b] = split_lanes(grad[b])
    for k in range(weights.shape[0]):
        value = weights[k]
        high = value.astype(jnp.bfloat16)
        rest = (value - high.astype(jnp.float32)).astype(jnp.bfloat16)
        column = jnp.concatenate([high, rest], axis=0)
        split_weights[:, pl.ds(k * LANES, LANES)] = jnp.concatenate([column, column], axis=1)

    for move in FACES + EDGES + CORNERS:
        back = tuple(-m for m in move)

        @pl.when(live[move] == 1)
        def _():
            copy_of(move).wait_send()

        @pl.when(live[back] == 1)
        def _():
            copy_of(move).wait_recv()


def conv_kernel(
    owner_dir, owner_slot, split_grad, face_in, edge_in, corner_in, features, active,
    split_weights, input_grad, partial, cube, windows, wide,
):
    blocks, channels, volume = features.shape
    taps = split_weights.shape[1] // LANES
    low_half = lax.broadcasted_iota(jnp.int32, (BS, LANES), 1) < LANES // 2
    wide[...] = jnp.zeros_like(wide)

    def cube_row(move):
        origin = CUBE_STEPS[0] + CUBE_STEPS[1] + BS
        return origin + sum(
            step * (BS if m == 1 else -1) for step, m in zip(CUBE_STEPS, move) if m != 0
        )

    def fill_own(offset, slot):
        back = tuple(-m for m in offset)
        source, into = side_row(back), cube_row(offset)
        free = free_axes(offset)
        if not free:
            cube[pl.ds(into, 1), :] = split_grad[slot, pl.ds(source, 1), :]
            return
        along = free[-1]
        for lead in itertools.product(range(BS), repeat=len(free) - 1):
            shift = sum(BLOCK_STEPS[a] * u for a, u in zip(free, lead))
            move = sum(CUBE_STEPS[a] * u for a, u in zip(free, lead))
            cube[pl.ds(into + move, BS, stride=CUBE_STEPS[along]), :] = split_grad[
                slot, pl.ds(source + shift, BS, stride=BLOCK_STEPS[along]), :
            ]

    def fill_remote(offset, owner, slot):
        group, f = place(tuple(-m for m in owner))
        into = cube_row(offset)
        picks = [BS - 1 if offset[a] == -1 else 0 for a in range(3)]
        if group == 2:
            value = jnp.where(low_half, corner_in[f, slot], 0.0)
            cube[pl.ds(into, 1), :] = split_lanes(value)[:1]
        elif group == 1:
            (along,) = free_axes(owner)
            value = split_lanes(jnp.where(low_half, edge_in[f, slot], 0.0))
            if offset[along] == 0:
                cube[pl.ds(into, BS, stride=CUBE_STEPS[along]), :] = value
            else:
                at = picks[along]
                cube[pl.ds(into, 1), :] = value[at : at + 1]
        else:
            first, second = free_axes(owner)
            for u in range(BS) if offset[first] == 0 else (picks[first],):
                half, row = divmod(u, BS // 2)
                value = face_in[f, slot, pl.ds(row * BS, BS), :]
                if half:
                    value = pltpu.roll(value, LANES // 2, 1)
                value = split_lanes(jnp.where(low_half, value, 0.0))
                at_u = into + (u * CUBE_STEPS[first] if offset[first] == 0 else 0)
                if offset[second] == 0:
                    cube[pl.ds(at_u, BS, stride=CUBE_STEPS[second]), :] = value
                else:
                    at = picks[second]
                    cube[pl.ds(at_u, 1), :] = value[at : at + 1]

    def visit_block(b, carry):
        cube[...] = jnp.zeros_like(cube)
        for x in range(BS):
            for y in range(BS):
                cube[pl.ds(cube_row((0, 0, 0)) + x * CUBE_STEPS[0] + y * CUBE_STEPS[1], BS), :] = (
                    split_grad[b, pl.ds((x * BS + y) * BS, BS), :]
                )
        for offset in HEADINGS:
            o = 9 * (offset[0] + 1) + 3 * (offset[1] + 1) + offset[2] + 1
            code, slot = owner_dir[b, o], owner_slot[b, o]

            @pl.when(code != 27)
            def _():
                @pl.when(code == 13)
                def _():
                    fill_own(offset, slot)

                for owner in itertools.product(*[(0,) if m == 0 else (0, m) for m in offset]):
                    if owner != (0, 0, 0):
                        @pl.when(code == 9 * (owner[0] + 1) + 3 * (owner[1] + 1) + owner[2] + 1)
                        def _():
                            fill_remote(offset, owner, slot)

        for ky in (-1, 0, 1):
            for kz in (-1, 0, 1):
                for x in range(BS + 2):
                    tiles = [
                        cube[pl.ds(x * CUBE_STEPS[0] + (y + 1 - ky) * CUBE_STEPS[1] + BS - kz, BS), :]
                        for y in range(BS)
                    ]
                    windows[3 * (ky + 1) + kz + 1, pl.ds(x * BS * BS, BS * BS), :] = (
                        jnp.concatenate(tiles, axis=0).astype(jnp.bfloat16)
                    )
        whole = jnp.concatenate(
            [
                windows[q, pl.ds((1 - kx) * BS * BS, volume), :]
                for kx in (-1, 0, 1)
                for q in range(9)
            ],
            axis=1,
        )
        mask = active[pl.ds(b, 1), :].astype(jnp.float32)
        result = lax.dot_general(
            whole, split_weights[...], (((1,), (1,)), ((), ())), preferred_element_type=jnp.float32
        )
        result = (result + pltpu.roll(result, LANES // 2, 1)).T
        input_grad[b] = result[:channels] * mask
        masked = features[b] * mask
        high = masked.astype(jnp.bfloat16)
        rest = (masked - high.astype(jnp.float32)).astype(jnp.bfloat16)
        wide[...] += jnp.dot(
            jnp.concatenate([high, rest], axis=0), whole, preferred_element_type=jnp.float32
        )
        return carry

    lax.fori_loop(0, blocks, visit_block, 0)
    half = lax.broadcasted_iota(jnp.int32, (channels, LANES), 1) < LANES // 2

    def summed(k):
        value = wide[:channels, pl.ds(k * LANES, LANES)] + wide[channels:, pl.ds(k * LANES, LANES)]
        return value + pltpu.roll(value, LANES // 2, 1)

    for pair in range((taps + 1) // 2):
        value = summed(2 * pair)
        other = summed(2 * pair + 1) if 2 * pair + 1 < taps else jnp.zeros_like(value)
        partial[pair] = jnp.where(half, value, other)


def shards(sizes, features, preact, cotangent, kernel, active, owner_dir, owner_slot, send_list):
    blocks, channels, volume = features.shape
    listed = send_list.shape[0]
    taps = kernel.shape[0]
    vmem = pl.BlockSpec(memory_space=pltpu.VMEM)
    smem = pl.BlockSpec(memory_space=pltpu.SMEM)
    shaped = jax.ShapeDtypeStruct
    rows = (BS * BS // 2, BS, BS)
    sheets = [(len(g), listed, r, LANES) for g, r in zip(GROUPS, rows)]
    split_grad, split_weights, bias, *landed = pl.pallas_call(
        functools.partial(halo_kernel, sizes),
        out_shape=[
            shaped((blocks, volume, LANES), jnp.float32),
            shaped((2 * channels, taps * LANES), jnp.bfloat16),
            shaped((BS, LANES), jnp.float32),
        ]
        + [shaped(s, jnp.float32) for s in sheets],
        in_specs=[smem, vmem, vmem, vmem, vmem],
        out_specs=[vmem] * 6,
        scratch_shapes=[
            pltpu.VMEM((blocks, volume, LANES), jnp.float32),
            pltpu.VMEM((volume, LANES), jnp.float32),
        ]
        + [pltpu.VMEM(s, jnp.float32) for s in sheets]
        + [pltpu.SemaphoreType.DMA((len(HEADINGS),))] * 2,
        compiler_params=pltpu.CompilerParams(
            collective_id=0, has_side_effects=True, vmem_limit_bytes=40 * 2**20
        ),
        name="halo",
    )(send_list, preact, cotangent, active, kernel)
    input_grad, partial = pl.pallas_call(
        conv_kernel,
        out_shape=[
            shaped((blocks, channels, volume), jnp.float32),
            shaped(((taps + 1) // 2, channels, LANES), jnp.float32),
        ],
        in_specs=[smem, smem] + [vmem] * 7,
        out_specs=[vmem] * 2,
        scratch_shapes=[
            pltpu.VMEM(((BS + 2) * CUBE_STEPS[0], LANES), jnp.float32),
            pltpu.VMEM((9, (BS + 2) * BS * BS, LANES), jnp.bfloat16),
            pltpu.VMEM((2 * channels, taps * LANES), jnp.float32),
        ],
        compiler_params=pltpu.CompilerParams(vmem_limit_bytes=48 * 2**20),
        name="conv",
    )(owner_dir, owner_slot, split_grad, *landed, features, active, split_weights)
    scaling = (volume * blocks * lax.axis_size(AXES)) ** (-0.5)
    total, bias_total = lax.psum((partial, bias), AXES)
    pairs = total.reshape(-1, channels, 2, channels).transpose(0, 2, 1, 3)
    kernel_grad = pairs.reshape(-1, channels, channels)[:taps] * scaling
    return input_grad, kernel_grad, bias_total[0, :channels] * scaling


def solution(mesh):
    whole = P(AXES, None, None)
    table = P(AXES, None)
    sizes = tuple(mesh.shape[axis] for axis in AXES)
    return jax.shard_map(
        functools.partial(shards, sizes),
        mesh=mesh,
        in_specs=(whole, whole, whole, P(), table, table, table, P(AXES)),
        out_specs=(whole, P(), P()),
        check_vma=False,
    )
```

time: 1880 us -> 170 us (0.09); the launches traced: 1860 us -> 169 us
  local copies, waits for them, and re-layouts: 816 us -> 6.61 us
  loops' own time: 706 us -> 0 us
  waiting for transfers between devices: 155 us -> 85.5 us
  other arithmetic: 70.3 us -> 1.6 us
  matrix products: 33.2 us -> 0 us
  Pallas kernels: 0 us -> 20.3 us
    another operation x1 -> x0, loops' own time: 706 us -> none  [shards(): lax.scan(visit_block, initial, (owner_dir, owner_slot, gradient, masked_i...]
    reshape x232 -> x0, local copies, waits for them, and re-layouts: 285 us -> none  [the longest x216 273 us: shifted_stack(): return jnp.stack(windows)]
    slice x316 -> x1, local copies, waits for them, and re-layouts: 261 us -> 1.35 us  [the longest x236 234 us: shifted_stack(): padded[:, begin_x:begin_x + extent, begin_y:begin_y + extent, begin_z:beg...]
    while x496 -> x0, local copies, waits for them, and re-layouts: 215 us -> none
    ppermute x6 -> x0, waiting for transfers between devices: 66.9 us -> none  [the longest x3 41.8 us: padded_2(): lax.ppermute(head, axis, [((i + 1) % count, i) for i in range(ends)])]
    select_n x97 -> x0, other arithmetic: 40.7 us -> none  [the longest x76 39.5 us: gather_cube(): jnp.where(code_here == code, remote_piece(sheet_row, owner_offset, block_...]
    dot_general x8 -> x0, matrix products: 33.2 us -> none  [the longest x4 20.7 us: visit_block(): jnp.einsum('kiv,ov->kio', input_windows, own_grad, precision=lax.Precisio...]
    dynamic_slice x28 -> x0, local copies, waits for them, and re-layouts: 30.2 us -> none  [the longest x20 22.6 us: gather_cube(): lax.dynamic_index_in_dim(sheets[owner_offset], remote_row[index], 0, keep...]
  transfers between devices with their start and end apart: 7 -> 1, of which waited for: 5 -> 1; matrix products, arithmetic and copies ran while one was open for 1% -> 0% of each run, Pallas kernels for 0% -> 0%
where the time goes in v1:
time: 170 us; the launch traced here: 169 us
  waiting for transfers between devices  85.5 us (50%)
  blocking collectives  40.6 us (24%)
  Pallas kernels  20.3 us (12%)
  between operations  14.1 us (8%)
  local copies, waits for them, and re-layouts  6.61 us (4%)
    psum x1, waiting for transfers between devices, shards(): total, bias_total = lax.psum((partial, bias), AXES)  85.5 us
    psum x1, blocking collectives, shards(): total, bias_total = lax.psum((partial, bias), AXES)  40.6 us
    pallas_call x1, Pallas kernels, shards(): pl.pallas_call(functools.partial(halo_kernel, sizes), out_shape=[shaped((...  10.2 us
    pallas_call x1, Pallas kernels, shards(): pl.pallas_call(conv_kernel, out_shape=[shaped((blocks, channels, volume),...  10.1 us
    unnamed x18, local copies, waits for them, and re-layouts  5.27 us
  transfers between devices with their start and end apart: 1, of which 1 were waited for; matrix products, arithmetic and copies ran while one was open for 0% of the time, Pallas kernels for 0%

profile of v1, /device:TPU:0, one launch (start us, length us, event | category | flops | bytes accessed | tf_op | source)
XLA Modules:
  0.0 168.8 jit_solution(6203083921497375969)
XLA Ops:
  7.2 0.0 all-reduce.2.cloned.1.call-start
  7.2 0.0 copy-start
  7.2 1.2 copy-done
  8.4 0.0 copy-start.1
  8.4 1.0 copy-done.1
  9.4 1.0 copy-done.2
  10.5 0.0 copy-start.4
  10.5 0.7 copy-done.4
  11.2 0.0 copy-start.8
  11.2 0.7 copy-done.8
  11.8 10.2 %halo.1 = (f32[4,512,128]{2,1,0:T(8,128)S(1)}, bf16[128,3456]{1,0:T(8,128)(2,1)S(1)}, f32[8,128]{1,0:T(8,128)S(1)}, f32[6,3,32,128]{3,2,1,0:T(8,128)S(1)}, f32[1...) custom-call(s32[3]{0:T(128)S(1)} %copy-done.8, f32[4,64,512]{2,1,0:T(8,128)S(1)} %copy-done.1, ...), custom_call_target="tpu_custom_call" | custom-call | tf_op jit(solution)/shard_map/halo/pallas_call | solution.py:282
  22.0 0.0 copy-start.5
  22.0 0.0 copy-done.3
  22.0 0.0 copy-done.6
  22.1 0.0 copy-done.7
  22.1 0.7 copy-done.5
  22.7 10.1 %conv.1 = (f32[4,64,512]{2,1,0:T(8,128)}, f32[14,64,128]{2,1,0:T(8,128)}) custom-call(s32[4,27]{1,0:T(4,128)S(1)} %copy-done.6, s32[4,27]{1,0:T(4,128)S(1)} %copy-done.7, f32[4,512,128]{2,1,0:T(8,128)S(1)} %get-tuple-element.11.split_grad, f32[6,3,32,128]{3,2,1,0:T(8,128)S(1)} %get-tuple-element.12.face_in, f32[12,3,8,128]{3,2,1,0:T(8,128)S(1)} %get-tuple-element.13.edge_in, ...), custom_call_target="tpu_custom_call" | custom-call | tf_op jit(solution)/shard_map/conv/pallas_call | solution.py:303
  32.8 0.0 all-reduce.2.cloned.1.call-update
  32.8 40.6 %psum.15 = f32[8,128]{1,0:T(8,128)S(1)} all-reduce(f32[8,128]{1,0:T(8,128)S(1)} %get-tuple-element.18), channel_id=1, replica_groups=mesh['gx'=4,'gy'=2,'gz'=4] {'gx','gy','gz'}, use_global_device_ids=true, to_apply=%region_1.0 | all-reduce | flops 1024 | bytes 8192 | tf_op jit(solution)/shard_map/psum | solution.py:320
  73.5 0.5 multiply_bitcast_fusion
  74.0 85.5 %all-reduce.2.cloned.1.call-done = f32[14,64,128]{2,1,0:T(8,128)} async-done(((f32[14,64,128]{2,1,0:T(8,128)}), f32[14,64,128]{2,1,0:T(8,128)}) %all-reduce.2.cloned.1.call-update) | async-done | bytes 458768 | tf_op jit(solution)/shard_map/psum | solution.py:320
  159.5 1.3 fusion
  160.8 0.1 pad_maximum_fusion
  160.9 1.0 slice_multiply_fusion
  (4 shorter events, 0.0 us)
Async XLA Ops:
  7.2 152.3 %all-reduce.2.cloned.1.call-start = ((), (), s32[]{:S(2)}) async-start(), calls=%async_computation | async-start | bytes 917504 | tf_op jit(solution)/shard_map/psum | solution.py:320
  7.2 1.2 copy-start
  8.4 1.0 copy-start.1
  9.4 1.0 copy-start.2
  10.5 0.7 copy-start.4
  11.2 0.7 copy-start.8
  11.8 10.2 %copy-start.3 = (f32[4,64,512]{2,1,0:T(8,128)S(1)}, f32[4,64,512]{2,1,0:T(8,128)}, u32[]{:S(2)}) copy-start(f32[4,64,512]{2,1,0:T(8,128)} %features.1) | copy-start | bytes 1572868
  11.8 10.2 %copy-start.6 = (s32[4,27]{1,0:T(4,128)S(1)}, s32[4,27]{1,0:T(4,128)}, u32[]{:S(2)}) copy-start(s32[4,27]{1,0:T(4,128)} %owner_dir.1) | copy-start | bytes 1300
  11.8 10.2 %copy-start.7 = (s32[4,27]{1,0:T(4,128)S(1)}, s32[4,27]{1,0:T(4,128)}, u32[]{:S(2)}) copy-start(s32[4,27]{1,0:T(4,128)} %owner_slot.1) | copy-start | bytes 1300
  22.0 0.7 copy-start.5
Sparse Core Ops, SparseCore 0:
  33.0 126.4 all-reduce.1

commit v2 on v1

--- a/solution.py
+++ b/solution.py
@@ -46,11 +46,23 @@
 
 
 def halo_kernel(
-    sizes, send_list, preact, cotangent, active, weights, split_grad, split_weights, bias,
-    face_in, edge_in, corner_in, grad, picked, face_out, edge_out, corner_out, send_sem, recv_sem,
+    sizes, send_list, preact_far, cotangent_far, active_far, split_grad,
+    bias, mask, face_in, edge_in, corner_in, grad, picked, preact, cotangent, active,
+    face_out, edge_out, corner_out, send_sem, recv_sem, fetch_sem,
 ):
     blocks, channels, volume = preact.shape
     listed = send_list.shape[0]
+    fetch_active = pltpu.make_async_copy(active_far, active, fetch_sem.at[2 * blocks])
+    fetches = [
+        [
+            pltpu.make_async_copy(far.at[b], near.at[b], fetch_sem.at[2 * b + n])
+            for n, (far, near) in enumerate(((preact_far, preact), (cotangent_far, cotangent)))
+        ]
+        for b in range(blocks)
+    ]
+    fetch_active.start()
+    for fetch in sum(fetches, []):
+        fetch.start()
     here = [lax.axis_index(axis) for axis in AXES]
 
     def inside(move):
@@ -71,8 +83,12 @@
             pl.semaphore_signal(barrier, inc=1, device_id=target[move], device_id_type=MESH)
 
     total = jnp.zeros((1, LANES), jnp.float32)
+    fetch_active.wait()
+    mask[...] = active[...].astype(jnp.float32)
     for b in range(blocks):
-        value = cotangent[b] * silu_slope(preact[b]) * active[pl.ds(b, 1), :].astype(jnp.float32)
+        for fetch in fetches[b]:
+            fetch.wait()
+        value = cotangent[b] * silu_slope(preact[b]) * mask[pl.ds(b, 1), :]
         rows = jnp.concatenate([value, jnp.zeros((LANES - channels, volume), jnp.float32)], axis=0).T
         grad[b] = rows
         total = total + jnp.sum(rows, axis=0, keepdims=True)
@@ -123,31 +139,31 @@
 
     for b in range(blocks):
         split_grad[b] = split_lanes(grad[b])
-    for k in range(weights.shape[0]):
+
+    for move in FACES + EDGES + CORNERS:
+        back = tuple(-m for m in move)
+
+        @pl.when(live[move] == 1)
+        def _():
+            copy_of(move).wait_send()
+
+        @pl.when(live[back] == 1)
+        def _():
+            copy_of(move).wait_recv()
+
+
+def conv_kernel(
+    owner_dir, owner_slot, split_grad, face_in, edge_in, corner_in, features, voxel_mask,
+    weights, bias, input_grad, partial, cube, windows, wide, split_weights,
+):
+    blocks, channels, volume = features.shape
+    taps = weights.shape[0]
+    for k in range(taps):
         value = weights[k]
         high = value.astype(jnp.bfloat16)
         rest = (value - high.astype(jnp.float32)).astype(jnp.bfloat16)
         column = jnp.concatenate([high, rest], axis=0)
         split_weights[:, pl.ds(k * LANES, LANES)] = jnp.concatenate([column, column], axis=1)
-
-    for move in FACES + EDGES + CORNERS:
-        back = tuple(-m for m in move)
-
-        @pl.when(live[move] == 1)
-        def _():
-            copy_of(move).wait_send()
-
-        @pl.when(live[back] == 1)
-        def _():
-            copy_of(move).wait_recv()
-
-
-def conv_kernel(
-    owner_dir, owner_slot, split_grad, face_in, edge_in, corner_in, features, active,
-    split_weights, input_grad, partial, cube, windows, wide,
-):
-    blocks, channels, volume = features.shape
-    taps = split_weights.shape[1] // LANES
     low_half = lax.broadcasted_iota(jnp.int32, (BS, LANES), 1) < LANES // 2
     wide[...] = jnp.zeros_like(wide)
 
@@ -243,7 +259,7 @@
             ],
             axis=1,
         )
-        mask = active[pl.ds(b, 1), :].astype(jnp.float32)
+        mask = voxel_mask[pl.ds(b, 1), :]
         result = lax.dot_general(
             whole, split_weights[...], (((1,), (1,)), ((), ())), preferred_element_type=jnp.float32
         )
@@ -264,10 +280,130 @@
         value = wide[:channels, pl.ds(k * LANES, LANES)] + wide[channels:, pl.ds(k * LANES, LANES)]
         return value + pltpu.roll(value, LANES // 2, 1)
 
+    tiles = channels // BS
+    spare = jnp.concatenate(
+        [pltpu.roll(bias[...], LANES // 2, 1), jnp.zeros((channels - BS, LANES), jnp.float32)], axis=0
+    )
+    pairs = (taps + 1) // 2
+    for pair in range(pairs):
+        value = summed(2 * pair)
+        other = summed(2 * pair + 1) if 2 * pair + 1 < taps else spare
+        partial[pl.ds(pair * tiles, tiles)] = jnp.where(half, value, other).reshape(tiles, BS, LANES)
+    if partial.shape[0] > pairs * tiles:
+        rest = partial.shape[0] - pairs * tiles
+        partial[pl.ds(pairs * tiles, rest)] = jnp.zeros((rest, BS, LANES), jnp.float32)
+
+
+def reduce_kernel(
+    sizes, chunks, partial, kernel_grad, bias_grad, arrived, line, full,
+    near_send, near_recv, line_send, line_recv, back_send, back_recv,
+):
+    here = [lax.axis_index(axis) for axis in AXES]
+    plane, depth = sizes[0] * sizes[1], sizes[2]
+    share = partial.shape[0] // (chunks * plane)
+    me = here[0] * sizes[1] + here[1]
+    peers = [lax.rem(me + j, plane) for j in range(plane)]
+    peer_at = [(p // sizes[1], lax.rem(p, sizes[1]), here[2]) for p in peers]
+    line_at = [(here[0], here[1], lax.rem(here[2] + j, depth)) for j in range(depth)]
+    barrier = pltpu.get_barrier_semaphore()
+    for device in peer_at[1:] + line_at[1:]:
+        pl.semaphore_signal(barrier, inc=1, device_id=device, device_id_type=MESH)
+    pl.semaphore_wait(barrier, plane + depth - 2)
+
+    def part(c, p):
+        return pl.ds((c * plane + p) * share, share)
+
+    def scatter(c, j):
+        return pltpu.make_async_remote_copy(
+            src_ref=partial.at[part(c, peers[j])],
+            dst_ref=arrived.at[c, j],
+            send_sem=near_send.at[c, j],
+            recv_sem=near_recv.at[c, j],
+            device_id=peer_at[j],
+            device_id_type=MESH,
+        )
+
+    def swap(c, j):
+        return pltpu.make_async_remote_copy(
+            src_ref=line.at[c, here[2]],
+            dst_ref=line.at[c, here[2]],
+            send_sem=line_send.at[c, j],
+            recv_sem=line_recv.at[c, j],
+            device_id=line_at[j],
+            device_id_type=MESH,
+        )
+
+    def gather(c, j):
+        return pltpu.make_async_remote_copy(
+            src_ref=full.at[part(c, me)],
+            dst_ref=full.at[part(c, me)],
+            send_sem=back_send.at[c, j],
+            recv_sem=back_recv.at[c, j],
+            device_id=peer_at[j],
+            device_id_type=MESH,
+        )
+
+    def landing(c, j):
+        behind = lax.rem(me + plane - j, plane)
+        return pltpu.make_async_remote_copy(
+            src_ref=full.at[part(c, behind)],
+            dst_ref=full.at[part(c, behind)],
+            send_sem=back_send.at[c, j],
+            recv_sem=back_recv.at[c, j],
+            device_id=peer_at[j],
+            device_id_type=MESH,
+        )
+
+    def line_landing(c, j):
+        behind = lax.rem(here[2] + depth - j, depth)
+        return pltpu.make_async_remote_copy(
+            src_ref=line.at[c, behind],
+            dst_ref=line.at[c, behind],
+            send_sem=line_send.at[c, j],
+            recv_sem=line_recv.at[c, j],
+            device_id=line_at[j],
+            device_id_type=MESH,
+        )
+
+    for c in range(chunks):
+        for j in range(1, plane):
+            scatter(c, j).start()
+    for c in range(chunks):
+        for j in range(1, plane):
+            scatter(c, j).wait_recv()
+        total = partial[part(c, me)]
+        for j in range(1, plane):
+            total = total + arrived[c, j]
+        line[c, here[2]] = total
+        for j in range(1, depth):
+            swap(c, j).start()
+    for c in range(chunks):
+        for j in range(1, depth):
+            line_landing(c, j).wait_recv()
+        total = line[c, 0]
+        for z in range(1, depth):
+            total = total + line[c, z]
+        full[part(c, me)] = total
+        for j in range(1, plane):
+            gather(c, j).start()
+    for c in range(chunks):
+        for j in range(1, plane):
+            landing(c, j).wait_recv()
+    taps, channels = kernel_grad.shape[:2]
+    tiles = channels // BS
     for pair in range((taps + 1) // 2):
-        value = summed(2 * pair)
-        other = summed(2 * pair + 1) if 2 * pair + 1 < taps else jnp.zeros_like(value)
-        partial[pair] = jnp.where(half, value, other)
+        value = full[pl.ds(pair * tiles, tiles)].reshape(channels, LANES)
+        kernel_grad[2 * pair] = value[:, :channels]
+        if 2 * pair + 1 < taps:
+            kernel_grad[2 * pair + 1] = pltpu.roll(value, LANES // 2, 1)[:, :channels]
+        else:
+            bias_grad[...] = pltpu.roll(value[:BS], LANES // 2, 1)
+    for c in range(chunks):
+        for j in range(1, plane):
+            scatter(c, j).wait_send()
+            gather(c, j).wait_send()
+        for j in range(1, depth):
+            swap(c, j).wait_send()
 
 
 def shards(sizes, features, preact, cotangent, kernel, active, owner_dir, owner_slot, send_list):
@@ -279,48 +415,69 @@
     shaped = jax.ShapeDtypeStruct
     rows = (BS * BS // 2, BS, BS)
     sheets = [(len(g), listed, r, LANES) for g, r in zip(GROUPS, rows)]
-    split_grad, split_weights, bias, *landed = pl.pallas_call(
+    far = pl.BlockSpec(memory_space=pltpu.HBM)
+    split_grad, bias, mask, *landed = pl.pallas_call(
         functools.partial(halo_kernel, sizes),
         out_shape=[
             shaped((blocks, volume, LANES), jnp.float32),
-            shaped((2 * channels, taps * LANES), jnp.bfloat16),
             shaped((BS, LANES), jnp.float32),
+            shaped(active.shape, jnp.float32),
         ]
         + [shaped(s, jnp.float32) for s in sheets],
-        in_specs=[smem, vmem, vmem, vmem, vmem],
+        in_specs=[smem, far, far, far],
         out_specs=[vmem] * 6,
         scratch_shapes=[
             pltpu.VMEM((blocks, volume, LANES), jnp.float32),
             pltpu.VMEM((volume, LANES), jnp.float32),
         ]
+        + [pltpu.VMEM(a.shape, a.dtype) for a in (preact, cotangent, active)]
         + [pltpu.VMEM(s, jnp.float32) for s in sheets]
-        + [pltpu.SemaphoreType.DMA((len(HEADINGS),))] * 2,
+        + [pltpu.SemaphoreType.DMA((len(HEADINGS),))] * 2
+        + [pltpu.SemaphoreType.DMA((2 * blocks + 1,))],
         compiler_params=pltpu.CompilerParams(
-            collective_id=0, has_side_effects=True, vmem_limit_bytes=40 * 2**20
+            collective_id=0, has_side_effects=True, vmem_limit_bytes=20 * 2**20
         ),
         name="halo",
-    )(send_list, preact, cotangent, active, kernel)
+    )(send_list, preact, cotangent, active)
+    plane, chunks = sizes[0] * sizes[1], 2
+    tiles = (taps + 1) // 2 * channels // BS
+    share = -(-tiles // (plane * chunks))
+    tiles = share * plane * chunks
     input_grad, partial = pl.pallas_call(
         conv_kernel,
         out_shape=[
             shaped((blocks, channels, volume), jnp.float32),
-            shaped(((taps + 1) // 2, channels, LANES), jnp.float32),
+            shaped((tiles, BS, LANES), jnp.float32),
         ],
-        in_specs=[smem, smem] + [vmem] * 7,
+        in_specs=[smem, smem] + [vmem] * 8,
         out_specs=[vmem] * 2,
         scratch_shapes=[
             pltpu.VMEM(((BS + 2) * CUBE_STEPS[0], LANES), jnp.float32),
             pltpu.VMEM((9, (BS + 2) * BS * BS, LANES), jnp.bfloat16),
             pltpu.VMEM((2 * channels, taps * LANES), jnp.float32),
+            pltpu.VMEM((2 * channels, taps * LANES), jnp.bfloat16),
         ],
-        compiler_params=pltpu.CompilerParams(vmem_limit_bytes=48 * 2**20),
+        compiler_params=pltpu.CompilerParams(vmem_limit_bytes=32 * 2**20),
         name="conv",
-    )(owner_dir, owner_slot, split_grad, *landed, features, active, split_weights)
+    )(owner_dir, owner_slot, split_grad, *landed, features, mask, kernel, bias)
+    total, bias_total = pl.pallas_call(
+        functools.partial(reduce_kernel, sizes, chunks),
+        out_shape=[shaped(kernel.shape, jnp.float32), shaped((BS, LANES), jnp.float32)],
+        in_specs=[vmem],
+        out_specs=[vmem] * 2,
+        scratch_shapes=[
+            pltpu.VMEM((chunks, plane, share, BS, LANES), jnp.float32),
+            pltpu.VMEM((chunks, sizes[2], share, BS, LANES), jnp.float32),
+            pltpu.VMEM((tiles, BS, LANES), jnp.float32),
+        ]
+        + [pltpu.SemaphoreType.DMA((chunks, n)) for n in (plane, plane, sizes[2], sizes[2], plane, plane)],
+        compiler_params=pltpu.CompilerParams(
+            collective_id=1, has_side_effects=True, vmem_limit_bytes=20 * 2**20
+        ),
+        name="reduce",
+    )(partial)
     scaling = (volume * blocks * lax.axis_size(AXES)) ** (-0.5)
-    total, bias_total = lax.psum((partial, bias), AXES)
-    pairs = total.reshape(-1, channels, 2, channels).transpose(0, 2, 1, 3)
-    kernel_grad = pairs.reshape(-1, channels, channels)[:taps] * scaling
-    return input_grad, kernel_grad, bias_total[0, :channels] * scaling
+    return input_grad, total * scaling, bias_total[0, :channels] * scaling
 
 
 def solution(mesh):

time: 170 us -> 49 us (0.29)
  waiting for transfers between devices: 85.5 us -> 0 us
  blocking collectives: 40.6 us -> 0 us
  Pallas kernels: 20.3 us -> 41.2 us
  between operations: 14.1 us -> 0.69 us
    psum x1 -> x0, waiting for transfers between devices: 85.5 us -> none  [shards(): total, bias_total = lax.psum((partial, bias), AXES)]
    psum x1 -> x0, blocking collectives: 40.6 us -> none  [shards(): total, bias_total = lax.psum((partial, bias), AXES)]
    pallas_call x0 -> x1, Pallas kernels: none -> 19.3 us  [shards(): pl.pallas_call(functools.partial(reduce_kernel, sizes, chunks), out_shape...]
    unnamed x18 -> x16, local copies, waits for them, and re-layouts: 5.27 us -> 5.22 us
  transfers between devices with their start and end apart: 1 -> 0, of which waited for: 1 -> 0; matrix products, arithmetic and copies ran while one was open for 0% -> 0% of each run, Pallas kernels for 0% -> 0%
where the time goes in v2:
time: 49 us; the launch traced here: 48.6 us
  Pallas kernels  41.2 us (84%)
  local copies, waits for them, and re-layouts  5.22 us (11%)
  other arithmetic  1.52 us (3%)
  between operations  0.69 us (1%)
    pallas_call x1, Pallas kernels, shards(): pl.pallas_call(functools.partial(reduce_kernel, sizes, chunks), out_shape...  19.3 us
    pallas_call x1, Pallas kernels, shards(): pl.pallas_call(functools.partial(halo_kernel, sizes), out_shape=[shaped((...  11.6 us
    pallas_call x1, Pallas kernels, shards(): pl.pallas_call(conv_kernel, out_shape=[shaped((blocks, channels, volume),...  10.3 us
    unnamed x16, local copies, waits for them, and re-layouts  5.22 us
    mul x2, other arithmetic, shards(): return (input_grad, total * scaling, bias_total[0, :channels] * scaling)  1.52 us

profile of v2, /device:TPU:0, one launch (start us, length us, event | category | flops | bytes accessed | tf_op | source)
XLA Modules:
  0.0 48.6 jit_solution(16079994259701494979)
XLA Ops:
  0.6 0.0 copy-start
  0.6 0.0 copy-start.1
  0.7 1.1 %copy-done.1 = f32[4,64,512]{2,1,0:T(8,128)S(1)} copy-done((f32[4,64,512]{2,1,0:T(8,128)S(1)}, f32[4,64,512]{2,1,0:T(8,128)}, u32[]{:S(2)}) %copy-start.1) | copy-done | bytes 524312
  1.8 0.0 copy-start.2
  1.8 1.0 %copy-done.2 = f32[4,64,512]{2,1,0:T(8,128)S(1)} copy-done((f32[4,64,512]{2,1,0:T(8,128)S(1)}, f32[4,64,512]{2,1,0:T(8,128)}, u32[]{:S(2)}) %copy-start.2) | copy-done | bytes 524312
  2.8 0.0 copy-start.4
  2.8 0.7 %copy-done.4 = s32[4,512]{1,0:T(4,128)S(1)} copy-done((s32[4,512]{1,0:T(4,128)S(1)}, s32[4,512]{1,0:T(4,128)}, u32[]{:S(2)}) %copy-start.4) | copy-done | bytes 8216
  3.5 0.0 copy-start.7
  3.5 0.7 %copy-done.7 = s32[3]{0:T(128)S(1)} copy-done((s32[3]{0:T(128)S(1)}, s32[3]{0:T(128)}, u32[]{:S(2)}) %copy-start.7) | copy-done | bytes 36
  4.2 11.6 %halo.1 = (f32[4,512,128]{2,1,0:T(8,128)S(1)}, f32[8,128]{1,0:T(8,128)S(1)}, f32[4,512]{1,0:T(4,128)S(1)}, f32[6,3,32,128]{3,2,1,0:T(8,128)S(1)}, f32[12,3,8,128...) custom-call(s32[3]{0:T(128)S(1)} %copy-done.7, f32[4,64,512]{2,1,0:T(8,128)S(1)} %copy-done.1, f32[4,64,512]{2,1,0:T(8,128)S(1)} %copy-done.2, ...), custom_call_target="tpu_custom_call" | custom-call | tf_op jit(solution)/shard_map/halo/pallas_call | solution.py:419
  15.8 0.0 copy-start.6
  15.8 0.0 copy-start.5
  15.8 0.0 copy-done
  15.8 0.7 %copy-done.6 = s32[4,27]{1,0:T(4,128)S(1)} copy-done((s32[4,27]{1,0:T(4,128)S(1)}, s32[4,27]{1,0:T(4,128)}, u32[]{:S(2)}) %copy-start.6) | copy-done | bytes 456
  16.5 0.0 copy-done.5
  16.5 0.0 copy-start.3
  16.5 1.0 %copy-done.3 = f32[4,64,512]{2,1,0:T(8,128)S(1)} copy-done((f32[4,64,512]{2,1,0:T(8,128)S(1)}, f32[4,64,512]{2,1,0:T(8,128)}, u32[]{:S(2)}) %copy-start.3) | copy-done | bytes 524312
  17.5 10.3 %conv.1 = (f32[4,64,512]{2,1,0:T(8,128)}, f32[112,8,128]{2,1,0:T(8,128)S(1)}) custom-call(s32[4,27]{1,0:T(4,128)S(1)} %copy-done.5, s32[4,27]{1,0:T(4,128)S(1)} %copy-done.6, f32[4,512,128]{2,1,0:T(8,128)S(1)} %get-tuple-element.13.split_grad, f32[6,3,32,128]{3,2,1,0:T(8,128)S(1)} %get-tuple-element.14.face_in, ...), custom_call_target="tpu_custom_call" | custom-call | tf_op jit(solution)/shard_map/conv/pallas_call | solution.py:446
  27.8 19.3 %reduce.1 = (f32[27,64,64]{2,1,0:T(8,128)S(1)}, f32[8,128]{1,0:T(8,128)S(1)}) custom-call(f32[112,8,128]{2,1,0:T(8,128)S(1)} %get-tuple-element.20.partial), custom_call_target="tpu_custom_call" | custom-call | tf_op jit(solution)/shard_map/reduce/pallas_call | solution.py:463
  47.1 1.0 %broadcast_multiply_fusion = f32[27,64,64]{2,1,0:T(8,128)} fusion(f32[27,64,64]{2,1,0:T(8,128)S(1)} %get-tuple-element.21), kind=kLoop, calls=%fused_computation | loop fusion | flops 110592 | bytes 884736 | tf_op jit(solution)/shard_map/mul | solution.py:480
  48.1 0.5 %multiply_bitcast_fusion = f32[64]{0:T(128)} fusion(f32[8,128]{1,0:T(8,128)S(1)} %get-tuple-element.22), kind=kLoop, calls=%fused_computation.1 | loop fusion | flops 64 | bytes 512 | tf_op jit(solution)/shard_map/mul | solution.py:480
Async XLA Ops:
  0.6 15.2 %copy-start = (f32[27,64,64]{2,1,0:T(8,128)S(1)}, f32[27,64,64]{2,1,0:T(8,128)}, u32[]{:S(2)}) copy-start(f32[27,64,64]{2,1,0:T(8,128)} %weights.1) | copy-start | bytes 1327108
  0.6 1.1 %copy-start.1 = (f32[4,64,512]{2,1,0:T(8,128)S(1)}, f32[4,64,512]{2,1,0:T(8,128)}, u32[]{:S(2)}) copy-start(f32[4,64,512]{2,1,0:T(8,128)} %preact_far.1) | copy-start | bytes 1572868
  1.8 1.0 %copy-start.2 = (f32[4,64,512]{2,1,0:T(8,128)S(1)}, f32[4,64,512]{2,1,0:T(8,128)}, u32[]{:S(2)}) copy-start(f32[4,64,512]{2,1,0:T(8,128)} %cotangent_far.1) | copy-start | bytes 1572868
  2.8 0.7 %copy-start.4 = (s32[4,512]{1,0:T(4,128)S(1)}, s32[4,512]{1,0:T(4,128)}, u32[]{:S(2)}) copy-start(s32[4,512]{1,0:T(4,128)} %active_far.1) | copy-start | bytes 24580
  3.5 0.7 %copy-start.7 = (s32[3]{0:T(128)S(1)}, s32[3]{0:T(128)}, u32[]{:S(2)}) copy-start(s32[3]{0:T(128)} %send_list.1) | copy-start | bytes 40
  15.8 0.7 %copy-start.6 = (s32[4,27]{1,0:T(4,128)S(1)}, s32[4,27]{1,0:T(4,128)}, u32[]{:S(2)}) copy-start(s32[4,27]{1,0:T(4,128)} %owner_slot.1) | copy-start | bytes 1300
  15.8 0.7 %copy-start.5 = (s32[4,27]{1,0:T(4,128)S(1)}, s32[4,27]{1,0:T(4,128)}, u32[]{:S(2)}) copy-start(s32[4,27]{1,0:T(4,128)} %owner_dir.1) | copy-start | bytes 1300
  16.5 1.0 %copy-start.3 = (f32[4,64,512]{2,1,0:T(8,128)S(1)}, f32[4,64,512]{2,1,0:T(8,128)}, u32[]{:S(2)}) copy-start(f32[4,64,512]{2,1,0:T(8,128)} %features.1) | copy-start | bytes 1572868

commit v3 on v1

--- a/solution.py
+++ b/solution.py
@@ -1,5 +1,6 @@
 import functools
 import itertools
+import math
 
 import jax
 import jax.numpy as jnp
@@ -46,11 +47,23 @@
 
 
 def halo_kernel(
-    sizes, send_list, preact, cotangent, active, weights, split_grad, split_weights, bias,
-    face_in, edge_in, corner_in, grad, picked, face_out, edge_out, corner_out, send_sem, recv_sem,
+    sizes, send_list, preact_far, cotangent_far, active_far, split_grad,
+    bias, mask, face_in, edge_in, corner_in, grad, picked, preact, cotangent, active,
+    face_out, edge_out, corner_out, send_sem, recv_sem, fetch_sem,
 ):
     blocks, channels, volume = preact.shape
     listed = send_list.shape[0]
+    fetch_active = pltpu.make_async_copy(active_far, active, fetch_sem.at[2 * blocks])
+    fetches = [
+        [
+            pltpu.make_async_copy(far.at[b], near.at[b], fetch_sem.at[2 * b + n])
+            for n, (far, near) in enumerate(((preact_far, preact), (cotangent_far, cotangent)))
+        ]
+        for b in range(blocks)
+    ]
+    fetch_active.start()
+    for fetch in sum(fetches, []):
+        fetch.start()
     here = [lax.axis_index(axis) for axis in AXES]
 
     def inside(move):
@@ -71,8 +84,12 @@
             pl.semaphore_signal(barrier, inc=1, device_id=target[move], device_id_type=MESH)
 
     total = jnp.zeros((1, LANES), jnp.float32)
+    fetch_active.wait()
+    mask[...] = active[...].astype(jnp.float32)
     for b in range(blocks):
-        value = cotangent[b] * silu_slope(preact[b]) * active[pl.ds(b, 1), :].astype(jnp.float32)
+        for fetch in fetches[b]:
+            fetch.wait()
+        value = cotangent[b] * silu_slope(preact[b]) * mask[pl.ds(b, 1), :]
         rows = jnp.concatenate([value, jnp.zeros((LANES - channels, volume), jnp.float32)], axis=0).T
         grad[b] = rows
         total = total + jnp.sum(rows, axis=0, keepdims=True)
@@ -123,12 +140,6 @@
 
     for b in range(blocks):
         split_grad[b] = split_lanes(grad[b])
-    for k in range(weights.shape[0]):
-        value = weights[k]
-        high = value.astype(jnp.bfloat16)
-        rest = (value - high.astype(jnp.float32)).astype(jnp.bfloat16)
-        column = jnp.concatenate([high, rest], axis=0)
-        split_weights[:, pl.ds(k * LANES, LANES)] = jnp.concatenate([column, column], axis=1)
 
     for move in FACES + EDGES + CORNERS:
         back = tuple(-m for m in move)
@@ -142,14 +153,11 @@
             copy_of(move).wait_recv()
 
 
-def conv_kernel(
-    owner_dir, owner_slot, split_grad, face_in, edge_in, corner_in, features, active,
-    split_weights, input_grad, partial, cube, windows, wide,
+def window_kernel(
+    owner_dir, owner_slot, split_grad, face_in, edge_in, corner_in, windows, cube
 ):
-    blocks, channels, volume = features.shape
-    taps = split_weights.shape[1] // LANES
+    blocks = split_grad.shape[0]
     low_half = lax.broadcasted_iota(jnp.int32, (BS, LANES), 1) < LANES // 2
-    wide[...] = jnp.zeros_like(wide)
 
     def cube_row(move):
         origin = CUBE_STEPS[0] + CUBE_STEPS[1] + BS
@@ -232,42 +240,197 @@
                         cube[pl.ds(x * CUBE_STEPS[0] + (y + 1 - ky) * CUBE_STEPS[1] + BS - kz, BS), :]
                         for y in range(BS)
                     ]
-                    windows[3 * (ky + 1) + kz + 1, pl.ds(x * BS * BS, BS * BS), :] = (
+                    windows[b, 3 * (ky + 1) + kz + 1, pl.ds(x * BS * BS, BS * BS), :] = (
                         jnp.concatenate(tiles, axis=0).astype(jnp.bfloat16)
                     )
-        whole = jnp.concatenate(
+        return carry
+
+    lax.fori_loop(0, blocks, visit_block, 0)
+
+
+def window(windows, b, k, volume):
+    kx, q = divmod(k, 9)
+    return windows[b, q, pl.ds((2 - kx) * BS * BS, volume), :]
+
+
+def conv_kernel(
+    sizes, chunks, windows, features, voxel_mask, weights, bias, input_grad, kernel_grad, bias_grad,
+    partial, full, split_weights, split_input, *rest,
+):
+    blocks, channels, volume = features.shape
+    taps = weights.shape[0]
+    here = [lax.axis_index(axis) for axis in AXES]
+    groups = stage_sizes(sizes)
+    stages = len(groups)
+    arrived, sums, sems = rest[:stages], rest[stages : 2 * stages], rest[2 * stages :]
+    pair = groups[0]
+    column, low = here[0] // pair, lax.rem(here[0], pair)
+    mine = (low, column * sizes[1] + here[1], here[2])
+
+    def member(g, j):
+        p = lax.rem(mine[g] + j, groups[g])
+        if g == 0:
+            return p, (column * pair + p, here[1], here[2])
+        if g == 1:
+            return p, (p // sizes[1] * pair + low, lax.rem(p, sizes[1]), here[2])
+        return p, (here[0], here[1], p)
+
+    lengths = [full.shape[1]]
+    for n in groups:
+        lengths.append(lengths[-1] // n)
+    bases = [0]
+    for g in range(stages):
+        bases.append(bases[-1] + mine[g] * lengths[g + 1])
+
+    barrier = pltpu.get_barrier_semaphore()
+    for g, n in enumerate(groups):
+        for j in range(1, n):
+            pl.semaphore_signal(barrier, inc=1, device_id=member(g, j)[1], device_id_type=MESH)
+
+    def scatter(c, g, j):
+        p, device = member(g, j)
+        source = partial.at[c] if g == 0 else sums[g - 1].at[c]
+        return pltpu.make_async_remote_copy(
+            src_ref=source.at[pl.ds(p * lengths[g + 1], lengths[g + 1])],
+            dst_ref=arrived[g].at[c, j],
+            send_sem=sems[4 * g].at[c, j],
+            recv_sem=sems[4 * g + 1].at[c, j],
+            device_id=device,
+            device_id_type=MESH,
+        )
+
+    def gather(c, g, j, place_of):
+        area = full.at[c, pl.ds(bases[g] + place_of * lengths[g + 1], lengths[g + 1])]
+        return pltpu.make_async_remote_copy(
+            src_ref=area,
+            dst_ref=area,
+            send_sem=sems[4 * g + 2].at[c, j],
+            recv_sem=sems[4 * g + 3].at[c, j],
+            device_id=member(g, j)[1],
+            device_id_type=MESH,
+        )
+
+    def start_scatter(c, g):
+        for j in range(1, groups[g]):
+            scatter(c, g, j).start()
+
+    def finish_scatter(c, g):
+        for j in range(1, groups[g]):
+            scatter(c, g, j).wait_recv()
+        own = pl.ds(mine[g] * lengths[g + 1], lengths[g + 1])
+        total = partial[c, own] if g == 0 else sums[g - 1][c, own]
+        for j in range(1, groups[g]):
+            total = total + arrived[g][c, j]
+        if g + 1 < stages:
+            sums[g][c] = total
+        else:
+            full[c, pl.ds(bases[stages], lengths[stages])] = total
+
+    def start_gather(c, g):
+        for j in range(1, groups[g]):
+            gather(c, g, j, mine[g]).start()
+
+    def finish_gather(c, g):
+        for j in range(1, groups[g]):
+            gather(c, g, j, lax.rem(mine[g] + groups[g] - j, groups[g])).wait_recv()
+
+    half = lax.broadcasted_iota(jnp.int32, (channels, LANES), 1) < LANES // 2
+    tiles = channels // BS
+    pairs = (taps + 1) // 2
+    per_chunk = full.shape[1] // tiles
+
+    for b in range(blocks):
+        masked = features[b] * voxel_mask[pl.ds(b, 1), :]
+        high = masked.astype(jnp.bfloat16)
+        low_part = (masked - high.astype(jnp.float32)).astype(jnp.bfloat16)
+        split_input[:, pl.ds(b * volume, volume)] = jnp.concatenate([high, low_part], axis=0)
+
+    def tap_pair(n):
+        span = [k for k in (2 * n, 2 * n + 1) if k < taps]
+        rows = jnp.concatenate(
             [
-                windows[q, pl.ds((1 - kx) * BS * BS, volume), :]
-                for kx in (-1, 0, 1)
-                for q in range(9)
+                jnp.concatenate([window(windows, b, k, volume) for k in span], axis=1)
+                for b in range(blocks)
             ],
-            axis=1,
+            axis=0,
         )
-        mask = active[pl.ds(b, 1), :].astype(jnp.float32)
+        wide = jnp.dot(split_input[...], rows, preferred_element_type=jnp.float32)
+        wide = wide[:channels] + wide[channels:]
+        parts = [wide[:, m * LANES : (m + 1) * LANES] for m in range(len(span))]
+        parts = [v + pltpu.roll(v, LANES // 2, 1) for v in parts]
+        if len(parts) == 1:
+            spare = jnp.zeros((channels - BS, LANES), jnp.float32)
+            parts.append(
+                jnp.concatenate([pltpu.roll(bias[...], LANES // 2, 1), spare], axis=0)
+            )
+        return jnp.where(half, *parts).reshape(tiles, BS, LANES)
+
+    def products(c):
+        for m in range(per_chunk):
+            n = c * per_chunk + m
+            partial[c, pl.ds(m * tiles, tiles)] = (
+                tap_pair(n) if n < pairs else jnp.zeros((tiles, BS, LANES), jnp.float32)
+            )
+
+    def input_block(b):
+        whole = jnp.concatenate([window(windows, b, k, volume) for k in range(taps)], axis=1)
         result = lax.dot_general(
             whole, split_weights[...], (((1,), (1,)), ((), ())), preferred_element_type=jnp.float32
         )
         result = (result + pltpu.roll(result, LANES // 2, 1)).T
-        input_grad[b] = result[:channels] * mask
-        masked = features[b] * mask
-        high = masked.astype(jnp.bfloat16)
-        rest = (masked - high.astype(jnp.float32)).astype(jnp.bfloat16)
-        wide[...] += jnp.dot(
-            jnp.concatenate([high, rest], axis=0), whole, preferred_element_type=jnp.float32
-        )
-        return carry
-
-    lax.fori_loop(0, blocks, visit_block, 0)
-    half = lax.broadcasted_iota(jnp.int32, (channels, LANES), 1) < LANES // 2
-
-    def summed(k):
-        value = wide[:channels, pl.ds(k * LANES, LANES)] + wide[channels:, pl.ds(k * LANES, LANES)]
-        return value + pltpu.roll(value, LANES // 2, 1)
-
-    for pair in range((taps + 1) // 2):
-        value = summed(2 * pair)
-        other = summed(2 * pair + 1) if 2 * pair + 1 < taps else jnp.zeros_like(value)
-        partial[pair] = jnp.where(half, value, other)
+        input_grad[b] = result[:channels] * voxel_mask[pl.ds(b, 1), :]
+
+    products(0)
+    pl.semaphore_wait(barrier, sum(groups) - stages)
+    start_scatter(0, 0)
+    for c in range(1, chunks):
+        products(c)
+        start_scatter(c, 0)
+
+    def prepare_weights():
+        for k in range(taps):
+            value = weights[k]
+            high = value.astype(jnp.bfloat16)
+            low_part = (value - high.astype(jnp.float32)).astype(jnp.bfloat16)
+            line = jnp.concatenate([high, low_part], axis=0)
+            split_weights[:, pl.ds(k * LANES, LANES)] = jnp.concatenate([line, line], axis=1)
+
+    queue = [prepare_weights] + [functools.partial(input_block, b) for b in range(blocks)]
+    for g in range(stages):
+        for c in range(chunks):
+            finish_scatter(c, g)
+            start_scatter(c, g + 1) if g + 1 < stages else start_gather(c, g)
+        for _ in range(2):
+            if queue:
+                queue.pop(0)()
+    for g in reversed(range(stages)):
+        for c in range(chunks):
+            finish_gather(c, g)
+            if g:
+                start_gather(c, g - 1)
+        if queue:
+            queue.pop(0)()
+    for work in queue:
+        work()
+
+    for n in range(pairs):
+        c, m = divmod(n, per_chunk)
+        value = full[c, pl.ds(m * tiles, tiles)].reshape(channels, LANES)
+        kernel_grad[2 * n] = value[:, :channels]
+        if 2 * n + 1 < taps:
+            kernel_grad[2 * n + 1] = pltpu.roll(value, LANES // 2, 1)[:, :channels]
+        else:
+            bias_grad[...] = pltpu.roll(value[:BS], LANES // 2, 1)
+    for g in range(stages):
+        for c in range(chunks):
+            for j in range(1, groups[g]):
+                scatter(c, g, j).wait_send()
+                gather(c, g, j, mine[g]).wait_send()
+
+
+def stage_sizes(sizes):
+    pair = 2 if sizes[0] % 2 == 0 else 1
+    return pair, sizes[0] // pair * sizes[1], sizes[2]
 
 
 def shards(sizes, features, preact, cotangent, kernel, active, owner_dir, owner_slot, send_list):
@@ -279,48 +442,71 @@
     shaped = jax.ShapeDtypeStruct
     rows = (BS * BS // 2, BS, BS)
     sheets = [(len(g), listed, r, LANES) for g, r in zip(GROUPS, rows)]
-    split_grad, split_weights, bias, *landed = pl.pallas_call(
+    far = pl.BlockSpec(memory_space=pltpu.HBM)
+    split_grad, bias, mask, *landed = pl.pallas_call(
         functools.partial(halo_kernel, sizes),
         out_shape=[
             shaped((blocks, volume, LANES), jnp.float32),
-            shaped((2 * channels, taps * LANES), jnp.bfloat16),
             shaped((BS, LANES), jnp.float32),
+            shaped(active.shape, jnp.float32),
         ]
         + [shaped(s, jnp.float32) for s in sheets],
-        in_specs=[smem, vmem, vmem, vmem, vmem],
+        in_specs=[smem, far, far, far],
         out_specs=[vmem] * 6,
         scratch_shapes=[
             pltpu.VMEM((blocks, volume, LANES), jnp.float32),
             pltpu.VMEM((volume, LANES), jnp.float32),
         ]
+        + [pltpu.VMEM(a.shape, a.dtype) for a in (preact, cotangent, active)]
         + [pltpu.VMEM(s, jnp.float32) for s in sheets]
-        + [pltpu.SemaphoreType.DMA((len(HEADINGS),))] * 2,
+        + [pltpu.SemaphoreType.DMA((len(HEADINGS),))] * 2
+        + [pltpu.SemaphoreType.DMA((2 * blocks + 1,))],
         compiler_params=pltpu.CompilerParams(
-            collective_id=0, has_side_effects=True, vmem_limit_bytes=40 * 2**20
+            collective_id=0, has_side_effects=True, vmem_limit_bytes=20 * 2**20
         ),
         name="halo",
-    )(send_list, preact, cotangent, active, kernel)
-    input_grad, partial = pl.pallas_call(
-        conv_kernel,
+    )(send_list, preact, cotangent, active)
+    windows = pl.pallas_call(
+        window_kernel,
+        out_shape=shaped((blocks, 9, (BS + 2) * BS * BS, LANES), jnp.bfloat16),
+        in_specs=[smem, smem] + [vmem] * 4,
+        out_specs=vmem,
+        scratch_shapes=[pltpu.VMEM(((BS + 2) * CUBE_STEPS[0], LANES), jnp.float32)],
+        compiler_params=pltpu.CompilerParams(vmem_limit_bytes=20 * 2**20),
+        name="windows",
+    )(owner_dir, owner_slot, split_grad, *landed)
+    groups, chunks = stage_sizes(sizes), 2
+    pair_tiles = channels // BS
+    step = chunks * math.lcm(math.prod(groups), pair_tiles)
+    tiles = -(-((taps + 1) // 2 * pair_tiles) // step) * step // chunks
+    lengths = [tiles]
+    for n in groups:
+        lengths.append(lengths[-1] // n)
+    input_grad, total, bias_total = pl.pallas_call(
+        functools.partial(conv_kernel, sizes, chunks),
         out_shape=[
-            shaped((blocks, channels, volume), jnp.float32),
-            shaped(((taps + 1) // 2, channels, LANES), jnp.float32),
+            shaped(features.shape, jnp.float32),
+            shaped(kernel.shape, jnp.float32),
+            shaped((BS, LANES), jnp.float32),
         ],
-        in_specs=[smem, smem] + [vmem] * 7,
-        out_specs=[vmem] * 2,
+        in_specs=[vmem] * 5,
+        out_specs=[vmem] * 3,
         scratch_shapes=[
-            pltpu.VMEM(((BS + 2) * CUBE_STEPS[0], LANES), jnp.float32),
-            pltpu.VMEM((9, (BS + 2) * BS * BS, LANES), jnp.bfloat16),
-            pltpu.VMEM((2 * channels, taps * LANES), jnp.float32),
-        ],
-        compiler_params=pltpu.CompilerParams(vmem_limit_bytes=48 * 2**20),
+            pltpu.VMEM((chunks, tiles, BS, LANES), jnp.float32),
+            pltpu.VMEM((chunks, tiles, BS, LANES), jnp.float32),
+            pltpu.VMEM((2 * channels, taps * LANES), jnp.bfloat16),
+            pltpu.VMEM((2 * channels, blocks * volume), jnp.bfloat16),
+        ]
+        + [pltpu.VMEM((chunks, n, m, BS, LANES), jnp.float32) for n, m in zip(groups, lengths[1:])]
+        + [pltpu.VMEM((chunks, m, BS, LANES), jnp.float32) for m in lengths[1:]]
+        + [pltpu.SemaphoreType.DMA((chunks, n)) for n in groups for _ in range(4)],
+        compiler_params=pltpu.CompilerParams(
+            collective_id=1, has_side_effects=True, vmem_limit_bytes=32 * 2**20
+        ),
         name="conv",
-    )(owner_dir, owner_slot, split_grad, *landed, features, active, split_weights)
+    )(windows, features, mask, kernel, bias)
     scaling = (volume * blocks * lax.axis_size(AXES)) ** (-0.5)
-    total, bias_total = lax.psum((partial, bias), AXES)
-    pairs = total.reshape(-1, channels, 2, channels).transpose(0, 2, 1, 3)
-    kernel_grad = pairs.reshape(-1, channels, channels)[:taps] * scaling
-    return input_grad, kernel_grad, bias_total[0, :channels] * scaling
+    return input_grad, total * scaling, bias_total[0, :channels] * scaling
 
 
 def solution(mesh):

time: 170 us -> 44.1 us (0.26)
  waiting for transfers between devices: 85.5 us -> 0 us
  blocking collectives: 40.6 us -> 0 us
  Pallas kernels: 20.3 us -> 35.8 us
  between operations: 14.1 us -> 0.7 us
    psum x1 -> x0, waiting for transfers between devices: 85.5 us -> none  [shards(): total, bias_total = lax.psum((partial, bias), AXES)]
    psum x1 -> x0, blocking collectives: 40.6 us -> none  [shards(): total, bias_total = lax.psum((partial, bias), AXES)]
    pallas_call x1 -> x2, Pallas kernels: 10.1 us -> 24.2 us  [the longest x1 21.6 us: shards(): pl.pallas_call(functools.partial(conv_kernel, sizes, chunks), out_shape=[...]
    unnamed x18 -> x17, local copies, waits for them, and re-layouts: 5.27 us -> 5.66 us
  transfers between devices with their start and end apart: 1 -> 0, of which waited for: 1 -> 0; matrix products, arithmetic and copies ran while one was open for 0% -> 0% of each run, Pallas kernels for 0% -> 0%
where the time goes in v3:
time: 44.1 us; the launch traced here: 43.7 us
  Pallas kernels  35.8 us (81%)
  local copies, waits for them, and re-layouts  5.66 us (13%)
  other arithmetic  1.49 us (3%)
  between operations  0.7 us (2%)
    pallas_call x1, Pallas kernels, shards(): pl.pallas_call(functools.partial(conv_kernel, sizes, chunks), out_shape=[...  21.6 us
    pallas_call x1, Pallas kernels, shards(): pl.pallas_call(functools.partial(halo_kernel, sizes), out_shape=[shaped((...  11.6 us
    unnamed x17, local copies, waits for them, and re-layouts  5.66 us
    pallas_call x1, Pallas kernels, shards(): pl.pallas_call(window_kernel, out_shape=shaped((blocks, 9, (BS + 2) * BS...  2.55 us
    mul x2, other arithmetic, shards(): return (input_grad, total * scaling, bias_total[0, :channels] * scaling)  1.49 us

profile of v3, /device:TPU:0, one launch (start us, length us, event | category | flops | bytes accessed | tf_op | source)
XLA Modules:
  0.0 43.7 jit_solution(8964899963680784390)
XLA Ops:
  0.6 0.0 copy-start
  0.6 0.0 copy-start.1
  0.7 1.1 %copy-done.1 = f32[4,64,512]{2,1,0:T(8,128)S(1)} copy-done((f32[4,64,512]{2,1,0:T(8,128)S(1)}, f32[4,64,512]{2,1,0:T(8,128)}, u32[]{:S(2)}) %copy-start.1) | copy-done | bytes 524312
  1.8 0.0 copy-start.2
  1.8 1.0 %copy-done.2 = f32[4,64,512]{2,1,0:T(8,128)S(1)} copy-done((f32[4,64,512]{2,1,0:T(8,128)S(1)}, f32[4,64,512]{2,1,0:T(8,128)}, u32[]{:S(2)}) %copy-start.2) | copy-done | bytes 524312
  2.8 0.0 copy-start.4
  2.8 0.7 %copy-done.4 = s32[4,512]{1,0:T(4,128)S(1)} copy-done((s32[4,512]{1,0:T(4,128)S(1)}, s32[4,512]{1,0:T(4,128)}, u32[]{:S(2)}) %copy-start.4) | copy-done | bytes 8216
  3.5 0.0 copy-start.7
  3.5 0.7 %copy-done.7 = s32[3]{0:T(128)S(1)} copy-done((s32[3]{0:T(128)S(1)}, s32[3]{0:T(128)}, u32[]{:S(2)}) %copy-start.7) | copy-done | bytes 36
  4.2 0.0 copy-start.3
  4.2 11.6 %halo.1 = (f32[4,512,128]{2,1,0:T(8,128)S(1)}, f32[8,128]{1,0:T(8,128)S(1)}, f32[4,512]{1,0:T(4,128)S(1)}, f32[6,3,32,128]{3,2,1,0:T(8,128)S(1)}, f32[12,3,8,128...) custom-call(s32[3]{0:T(128)S(1)} %copy-done.7, f32[4,64,512]{2,1,0:T(8,128)S(1)} %copy-done.1, f32[4,64,512]{2,1,0:T(8,128)S(1)} %copy-done.2, ...), custom_call_target="tpu_custom_call" | custom-call | tf_op jit(solution)/shard_map/halo/pallas_call | solution.py:446
  15.8 0.0 copy-start.5
  15.8 0.7 %copy-done.5 = s32[4,27]{1,0:T(4,128)S(1)} copy-done((s32[4,27]{1,0:T(4,128)S(1)}, s32[4,27]{1,0:T(4,128)}, u32[]{:S(2)}) %copy-start.5) | copy-done | bytes 456
  16.5 0.0 copy-start.6
  16.5 0.7 %copy-done.6 = s32[4,27]{1,0:T(4,128)S(1)} copy-done((s32[4,27]{1,0:T(4,128)S(1)}, s32[4,27]{1,0:T(4,128)}, u32[]{:S(2)}) %copy-start.6) | copy-done | bytes 456
  17.2 2.5 %windows.1 = bf16[4,9,640,128]{3,2,1,0:T(8,128)(2,1)S(1)} custom-call(s32[4,27]{1,0:T(4,128)S(1)} %copy-done.5, s32[4,27]{1,0:T(4,128)S(1)} %copy-done.6, f32[4,512,128]{2,1,0:T(8,128)S(1)} %get-tuple-element.12.split_grad, f32[6,3,32,128]{3,2,1,0:T(8,128)S(1)} %get-tuple-element.13.face_in, f32[12,3,8,128]{3,2,1,0:T(8,128)S(1)} %get-tuple-element.14.edge_in, ...), custom_call_target="tpu_custom_call" | custom-call | tf_op jit(solution)/shard_map/windows/pallas_call | solution.py:469
  19.7 0.0 copy-done
  19.7 0.0 copy-done.3
  19.7 21.6 %conv.1 = (f32[4,64,512]{2,1,0:T(8,128)S(1)}, f32[27,64,64]{2,1,0:T(8,128)S(1)}, f32[8,128]{1,0:T(8,128)S(1)}) custom-call(bf16[4,9,640,128]{3,2,1,0:T(8,128)(2,1)S(1)} %windows.1, f32[4,64,512]{2,1,0:T(8,128)S(1)} %copy-done.3, f32[4,512]{1,0:T(4,128)S(1)} %get-tuple-element.16.voxel_mask, f32[27,64,64]{2,1,0:T(8,128)S(1)} %copy-done, ...), custom_call_target="tpu_custom_call" | custom-call | tf_op jit(solution)/shard_map/conv/pallas_call | solution.py:485
  41.4 0.5 %multiply_bitcast_fusion = f32[64]{0:T(128)} fusion(f32[8,128]{1,0:T(8,128)S(1)} %get-tuple-element.20), kind=kLoop, calls=%fused_computation.1 | loop fusion | flops 64 | bytes 512 | tf_op jit(solution)/shard_map/mul | solution.py:509
  41.9 1.0 %broadcast_multiply_fusion = f32[27,64,64]{2,1,0:T(8,128)} fusion(f32[27,64,64]{2,1,0:T(8,128)S(1)} %get-tuple-element.19), kind=kLoop, calls=%fused_computation | loop fusion | flops 110592 | bytes 884736 | tf_op jit(solution)/shard_map/mul | solution.py:509
  42.9 0.8 %copy.12 = f32[4,64,512]{2,1,0:T(8,128)} copy(f32[4,64,512]{2,1,0:T(8,128)S(1)} %get-tuple-element.24) | data formatting | bytes 1048576
Async XLA Ops:
  0.6 19.1 %copy-start = (f32[27,64,64]{2,1,0:T(8,128)S(1)}, f32[27,64,64]{2,1,0:T(8,128)}, u32[]{:S(2)}) copy-start(f32[27,64,64]{2,1,0:T(8,128)} %weights.1) | copy-start | bytes 1327108
  0.6 1.1 %copy-start.1 = (f32[4,64,512]{2,1,0:T(8,128)S(1)}, f32[4,64,512]{2,1,0:T(8,128)}, u32[]{:S(2)}) copy-start(f32[4,64,512]{2,1,0:T(8,128)} %preact_far.1) | copy-start | bytes 1572868
  1.8 1.0 %copy-start.2 = (f32[4,64,512]{2,1,0:T(8,128)S(1)}, f32[4,64,512]{2,1,0:T(8,128)}, u32[]{:S(2)}) copy-start(f32[4,64,512]{2,1,0:T(8,128)} %cotangent_far.1) | copy-start | bytes 1572868
  2.8 0.7 %copy-start.4 = (s32[4,512]{1,0:T(4,128)S(1)}, s32[4,512]{1,0:T(4,128)}, u32[]{:S(2)}) copy-start(s32[4,512]{1,0:T(4,128)} %active_far.1) | copy-start | bytes 24580
  3.5 0.7 %copy-start.7 = (s32[3]{0:T(128)S(1)}, s32[3]{0:T(128)}, u32[]{:S(2)}) copy-start(s32[3]{0:T(128)} %send_list.1) | copy-start | bytes 40
  4.2 15.6 %copy-start.3 = (f32[4,64,512]{2,1,0:T(8,128)S(1)}, f32[4,64,512]{2,1,0:T(8,128)}, u32[]{:S(2)}) copy-start(f32[4,64,512]{2,1,0:T(8,128)} %features.1) | copy-start | bytes 1572868
  15.8 0.7 %copy-start.5 = (s32[4,27]{1,0:T(4,128)S(1)}, s32[4,27]{1,0:T(4,128)}, u32[]{:S(2)}) copy-start(s32[4,27]{1,0:T(4,128)} %owner_dir.1) | copy-start | bytes 1300
  16.5 0.7 %copy-start.6 = (s32[4,27]{1,0:T(4,128)S(1)}, s32[4,27]{1,0:T(4,128)}, u32[]{:S(2)}) copy-start(s32[4,27]{1,0:T(4,128)} %owner_slot.1) | copy-start | bytes 1300

commit v4 on v3

--- a/solution.py
+++ b/solution.py
@@ -95,6 +95,7 @@
         total = total + jnp.sum(rows, axis=0, keepdims=True)
     bias[...] = jnp.broadcast_to(total, bias.shape)
 
+    corner_out[...] = jnp.zeros_like(corner_out)
     for s in range(listed):
         entry = send_list[s]
         keep = (entry < blocks).astype(jnp.float32)
@@ -114,7 +115,7 @@
             (along,) = free_axes(move)
             edge_out[f, s] = picked[pl.ds(side_row(move), BS, stride=BLOCK_STEPS[along]), :]
         for f, move in enumerate(CORNERS):
-            corner_out[f, s] = jnp.broadcast_to(picked[pl.ds(side_row(move), 1), :], (BS, LANES))
+            corner_out[f, pl.ds(s, 1), :] = picked[pl.ds(side_row(move), 1), :]
 
     count = functools.reduce(lambda a, b: a + b, [live[move] for move in HEADINGS])
     pl.semaphore_wait(barrier, count)
@@ -185,8 +186,8 @@
         into = cube_row(offset)
         picks = [BS - 1 if offset[a] == -1 else 0 for a in range(3)]
         if group == 2:
-            value = jnp.where(low_half, corner_in[f, slot], 0.0)
-            cube[pl.ds(into, 1), :] = split_lanes(value)[:1]
+            value = jnp.where(low_half[:1], corner_in[f, pl.ds(slot, 1), :], 0.0)
+            cube[pl.ds(into, 1), :] = split_lanes(value)
         elif group == 1:
             (along,) = free_axes(owner)
             value = split_lanes(jnp.where(low_half, edge_in[f, slot], 0.0))
@@ -254,8 +255,8 @@
 
 
 def conv_kernel(
-    sizes, chunks, windows, features, voxel_mask, weights, bias, input_grad, kernel_grad, bias_grad,
-    partial, full, split_weights, split_input, *rest,
+    sizes, chunks, windows, features, voxel_mask, weights, bias, input_grad, full,
+    partial, split_weights, split_input, *rest,
 ):
     blocks, channels, volume = features.shape
     taps = weights.shape[0]
@@ -413,14 +414,6 @@
     for work in queue:
         work()
 
-    for n in range(pairs):
-        c, m = divmod(n, per_chunk)
-        value = full[c, pl.ds(m * tiles, tiles)].reshape(channels, LANES)
-        kernel_grad[2 * n] = value[:, :channels]
-        if 2 * n + 1 < taps:
-            kernel_grad[2 * n + 1] = pltpu.roll(value, LANES // 2, 1)[:, :channels]
-        else:
-            bias_grad[...] = pltpu.roll(value[:BS], LANES // 2, 1)
     for g in range(stages):
         for c in range(chunks):
             for j in range(1, groups[g]):
@@ -428,9 +421,30 @@
                 gather(c, g, j, mine[g]).wait_send()
 
 
+def finish_kernel(scaling, full, result, input_grad, kernel_grad, bias_grad, sem):
+    copy = pltpu.make_async_copy(result, input_grad, sem.at[0])
+    copy.start()
+    taps, channels = kernel_grad.shape[:2]
+    tiles = channels // BS
+    per_chunk = full.shape[1] // tiles
+    for n in range((taps + 1) // 2):
+        c, m = divmod(n, per_chunk)
+        value = full[c, pl.ds(m * tiles, tiles)].reshape(channels, LANES) * scaling
+        kernel_grad[2 * n] = value[:, :channels]
+        if 2 * n + 1 < taps:
+            kernel_grad[2 * n + 1] = pltpu.roll(value, LANES // 2, 1)[:, :channels]
+        else:
+            bias_grad[...] = pltpu.roll(value[:BS], LANES // 2, 1)[:1, :channels]
+    copy.wait()
+
+
 def stage_sizes(sizes):
     pair = 2 if sizes[0] % 2 == 0 else 1
     return pair, sizes[0] // pair * sizes[1], sizes[2]
+
+
+def in_hbm(array):
+    return pltpu.with_memory_space_constraint(array, pltpu.HBM)
 
 
 def shards(sizes, features, preact, cotangent, kernel, active, owner_dir, owner_slot, send_list):
@@ -442,6 +456,7 @@
     shaped = jax.ShapeDtypeStruct
     rows = (BS * BS // 2, BS, BS)
     sheets = [(len(g), listed, r, LANES) for g, r in zip(GROUPS, rows)]
+    sheets[2] = (len(CORNERS), -(-listed // BS) * BS, LANES)
     far = pl.BlockSpec(memory_space=pltpu.HBM)
     split_grad, bias, mask, *landed = pl.pallas_call(
         functools.partial(halo_kernel, sizes),
@@ -465,7 +480,7 @@
             collective_id=0, has_side_effects=True, vmem_limit_bytes=20 * 2**20
         ),
         name="halo",
-    )(send_list, preact, cotangent, active)
+    )(*[in_hbm(a) for a in (send_list, preact, cotangent, active)])
     windows = pl.pallas_call(
         window_kernel,
         out_shape=shaped((blocks, 9, (BS + 2) * BS * BS, LANES), jnp.bfloat16),
@@ -474,7 +489,7 @@
         scratch_shapes=[pltpu.VMEM(((BS + 2) * CUBE_STEPS[0], LANES), jnp.float32)],
         compiler_params=pltpu.CompilerParams(vmem_limit_bytes=20 * 2**20),
         name="windows",
-    )(owner_dir, owner_slot, split_grad, *landed)
+    )(in_hbm(owner_dir), in_hbm(owner_slot), split_grad, *landed)
     groups, chunks = stage_sizes(sizes), 2
     pair_tiles = channels // BS
     step = chunks * math.lcm(math.prod(groups), pair_tiles)
@@ -482,17 +497,15 @@
     lengths = [tiles]
     for n in groups:
         lengths.append(lengths[-1] // n)
-    input_grad, total, bias_total = pl.pallas_call(
+    result, full = pl.pallas_call(
         functools.partial(conv_kernel, sizes, chunks),
         out_shape=[
             shaped(features.shape, jnp.float32),
-            shaped(kernel.shape, jnp.float32),
-            shaped((BS, LANES), jnp.float32),
+            shaped((chunks, tiles, BS, LANES), jnp.float32),
         ],
         in_specs=[vmem] * 5,
-        out_specs=[vmem] * 3,
+        out_specs=[vmem] * 2,
         scratch_shapes=[
-            pltpu.VMEM((chunks, tiles, BS, LANES), jnp.float32),
             pltpu.VMEM((chunks, tiles, BS, LANES), jnp.float32),
             pltpu.VMEM((2 * channels, taps * LANES), jnp.bfloat16),
             pltpu.VMEM((2 * channels, blocks * volume), jnp.bfloat16),
@@ -506,7 +519,20 @@
         name="conv",
     )(windows, features, mask, kernel, bias)
     scaling = (volume * blocks * lax.axis_size(AXES)) ** (-0.5)
-    return input_grad, total * scaling, bias_total[0, :channels] * scaling
+    input_grad, kernel_grad, bias_grad = pl.pallas_call(
+        functools.partial(finish_kernel, scaling),
+        out_shape=[
+            shaped(features.shape, jnp.float32),
+            shaped(kernel.shape, jnp.float32),
+            shaped((1, channels), jnp.float32),
+        ],
+        in_specs=[vmem, pl.BlockSpec(memory_space=pl.ANY)],
+        out_specs=[pl.BlockSpec(memory_space=pl.ANY), vmem, vmem],
+        scratch_shapes=[pltpu.SemaphoreType.DMA((1,))],
+        compiler_params=pltpu.CompilerParams(vmem_limit_bytes=16 * 2**20),
+        name="finish",
+    )(full, result)
+    return input_grad, kernel_grad, bias_grad.reshape(channels)
 
 
 def solution(mesh):

time: 44.1 us -> 37.6 us (0.85)
  local copies, waits for them, and re-layouts: 5.66 us -> 0.01 us
  other arithmetic: 1.49 us -> 0 us
  Pallas kernels: 35.8 us -> 36.7 us
    unnamed x17 -> x4, local copies, waits for them, and re-layouts: 5.66 us -> 0.01 us
    pallas_call x0 -> x1, Pallas kernels: none -> 1.74 us  [shards(): pl.pallas_call(functools.partial(finish_kernel, scaling), out_shape=[shap...]
    mul x2 -> x0, other arithmetic: 1.49 us -> none  [shards(): return (input_grad, total * scaling, bias_total[0, :channels] * scaling)]
    pallas_call x1, Pallas kernels: 11.6 us -> 10.6 us  [shards(): pl.pallas_call(functools.partial(halo_kernel, sizes), out_shape=[shaped((...]
where the time goes in v4:
time: 37.6 us; the launch traced here: 37.4 us
  Pallas kernels  36.7 us (98%)
  between operations  0.69 us (2%)
    pallas_call x1, Pallas kernels, shards(): pl.pallas_call(functools.partial(conv_kernel, sizes, chunks), out_shape=[...  21.9 us
    pallas_call x1, Pallas kernels, shards(): pl.pallas_call(functools.partial(halo_kernel, sizes), out_shape=[shaped((...  10.6 us
    pallas_call x1, Pallas kernels, shards(): pl.pallas_call(window_kernel, out_shape=shaped((blocks, 9, (BS + 2) * BS...  2.49 us
    pallas_call x1, Pallas kernels, shards(): pl.pallas_call(functools.partial(finish_kernel, scaling), out_shape=[shap...  1.74 us

profile of v4, /device:TPU:0, one launch (start us, length us, event | category | flops | bytes accessed | tf_op | source)
XLA Modules:
  0.0 37.4 jit_solution(9027582630385178371)
XLA Ops:
  0.6 0.0 copy-start
  0.6 0.0 copy-start.1
  0.7 10.6 %halo.1 = (f32[4,512,128]{2,1,0:T(8,128)S(1)}, f32[8,128]{1,0:T(8,128)S(1)}, f32[4,512]{1,0:T(4,128)S(1)}, f32[6,3,32,128]{3,2,1,0:T(8,128)S(1)}, f32[12,3,8,128...) custom-call(s32[3]{0:T(128)} %send_list.1, f32[4,64,512]{2,1,0:T(8,128)} %preact_far.1, f32[4,64,512]{2,1,0:T(8,128)} %cotangent_far.1, ...), custom_call_target="tpu_custom_call" | custom-call | tf_op jit(solution)/shard_map/halo/pallas_call | solution.py:461
  11.2 2.5 %windows.1 = bf16[4,9,640,128]{3,2,1,0:T(8,128)(2,1)S(1)} custom-call(s32[4,27]{1,0:T(4,128)} %owner_dir.1, s32[4,27]{1,0:T(4,128)} %owner_slot.1, f32[4,512,128]{2,1,0:T(8,128)S(1)} %get-tuple-element.14.split_grad, f32[6,3,32,128]{3,2,1,0:T(8,128)S(1)} %get-tuple-element.15.face_in, f32[12,3,8,128]{3,2,1,0:T(8,128)S(1)} %get-tuple-element.16.edge_in, ...), custom_call_target="tpu_custom_call" | custom-call | tf_op jit(solution)/shard_map/windows/pallas_call | solution.py:484
  13.7 0.0 copy-done
  13.7 0.0 copy-done.1
  13.7 21.9 %conv.1 = (f32[4,64,512]{2,1,0:T(8,128)S(1)}, f32[2,64,8,128]{3,2,1,0:T(8,128)S(1)}) custom-call(bf16[4,9,640,128]{3,2,1,0:T(8,128)(2,1)S(1)} %windows.1, f32[4,64,512]{2,1,0:T(8,128)S(1)} %copy-done.1, f32[4,512]{1,0:T(4,128)S(1)} %get-tuple-element.18.voxel_mask, f32[27,64,64]{2,1,0:T(8,128)S(1)} %copy-done, f32[8,128]{1,0:T(8,128)S(1)} %get-tuple-element.19.bias), custom_call_target="tpu_custom_call" | custom-call | tf_op jit(solution)/shard_map/conv/pallas_call | solution.py:500
  35.7 1.7 %finish.1 = (f32[4,64,512]{2,1,0:T(8,128)}, f32[27,64,64]{2,1,0:T(8,128)}, f32[1,64]{1,0:T(1,128)}) custom-call(f32[2,64,8,128]{3,2,1,0:T(8,128)S(1)} %get-tuple-element.20.full, f32[4,64,512]{2,1,0:T(8,128)S(1)} %get-tuple-element.21.result), custom_call_target="tpu_custom_call" | custom-call | tf_op jit(solution)/shard_map/finish/pallas_call | solution.py:522
Async XLA Ops:
  0.6 13.1 %copy-start = (f32[27,64,64]{2,1,0:T(8,128)S(1)}, f32[27,64,64]{2,1,0:T(8,128)}, u32[]{:S(2)}) copy-start(f32[27,64,64]{2,1,0:T(8,128)} %weights.1) | copy-start | bytes 1327108
  0.6 13.1 %copy-start.1 = (f32[4,64,512]{2,1,0:T(8,128)S(1)}, f32[4,64,512]{2,1,0:T(8,128)}, u32[]{:S(2)}) copy-start(f32[4,64,512]{2,1,0:T(8,128)} %features.1) | copy-start | bytes 1572868

commit v5 on v4

--- a/solution.py
+++ b/solution.py
@@ -381,12 +381,15 @@
         result = (result + pltpu.roll(result, LANES // 2, 1)).T
         input_grad[b] = result[:channels] * voxel_mask[pl.ds(b, 1), :]
 
-    products(0)
-    pl.semaphore_wait(barrier, sum(groups) - stages)
-    start_scatter(0, 0)
-    for c in range(1, chunks):
-        products(c)
-        start_scatter(c, 0)
+    def advance(c, step):
+        if step < stages:
+            finish_scatter(c, step)
+            start_scatter(c, step + 1) if step + 1 < stages else start_gather(c, step)
+        else:
+            g = 2 * stages - 1 - step
+            finish_gather(c, g)
+            if g:
+                start_gather(c, g - 1)
 
     def prepare_weights():
         for k in range(taps):
@@ -397,20 +400,17 @@
             split_weights[:, pl.ds(k * LANES, LANES)] = jnp.concatenate([line, line], axis=1)
 
     queue = [prepare_weights] + [functools.partial(input_block, b) for b in range(blocks)]
-    for g in range(stages):
+    for step in range(chunks + 2 * stages):
+        if step < chunks:
+            products(step)
+            if step == 0:
+                pl.semaphore_wait(barrier, sum(groups) - stages)
+            start_scatter(step, 0)
+        elif queue:
+            queue.pop(0)()
         for c in range(chunks):
-            finish_scatter(c, g)
-            start_scatter(c, g + 1) if g + 1 < stages else start_gather(c, g)
-        for _ in range(2):
-            if queue:
-                queue.pop(0)()
-    for g in reversed(range(stages)):
-        for c in range(chunks):
-            finish_gather(c, g)
-            if g:
-                start_gather(c, g - 1)
-        if queue:
-            queue.pop(0)()
+            if 0 <= step - 1 - c < 2 * stages:
+                advance(c, step - 1 - c)
     for work in queue:
         work()
 
@@ -490,7 +490,8 @@
         compiler_params=pltpu.CompilerParams(vmem_limit_bytes=20 * 2**20),
         name="windows",
     )(in_hbm(owner_dir), in_hbm(owner_slot), split_grad, *landed)
-    groups, chunks = stage_sizes(sizes), 2
+    groups = stage_sizes(sizes)
+    chunks = min(4, max(1, 2 * channels // math.prod(groups)))
     pair_tiles = channels // BS
     step = chunks * math.lcm(math.prod(groups), pair_tiles)
     tiles = -(-((taps + 1) // 2 * pair_tiles) // step) * step // chunks

time: 37.6 us -> 46.8 us (1.24)
  Pallas kernels: 36.7 us -> 45.8 us
    pallas_call x1, Pallas kernels: 21.9 us -> 31 us  [shards(): pl.pallas_call(functools.partial(conv_kernel, sizes, chunks), out_shape=[...]
where the time goes in v5:
time: 46.8 us; the launch traced here: 46.5 us
  Pallas kernels  45.8 us (98%)
  between operations  0.69 us (1%)
    pallas_call x1, Pallas kernels, shards(): pl.pallas_call(functools.partial(conv_kernel, sizes, chunks), out_shape=[...  31 us
    pallas_call x1, Pallas kernels, shards(): pl.pallas_call(functools.partial(halo_kernel, sizes), out_shape=[shaped((...  10.6 us
    pallas_call x1, Pallas kernels, shards(): pl.pallas_call(window_kernel, out_shape=shaped((blocks, 9, (BS + 2) * BS...  2.49 us
    pallas_call x1, Pallas kernels, shards(): pl.pallas_call(functools.partial(finish_kernel, scaling), out_shape=[shap...  1.74 us

profile of v5, /device:TPU:0, one launch (start us, length us, event | category | flops | bytes accessed | tf_op | source)
XLA Modules:
  0.0 46.5 jit_solution(18384140072697220805)
XLA Ops:
  0.6 0.0 copy-start
  0.6 0.0 copy-start.1
  0.7 10.6 %halo.1 = (f32[4,512,128]{2,1,0:T(8,128)S(1)}, f32[8,128]{1,0:T(8,128)S(1)}, f32[4,512]{1,0:T(4,128)S(1)}, f32[6,3,32,128]{3,2,1,0:T(8,128)S(1)}, f32[12,3,8,128...) custom-call(s32[3]{0:T(128)} %send_list.1, f32[4,64,512]{2,1,0:T(8,128)} %preact_far.1, f32[4,64,512]{2,1,0:T(8,128)} %cotangent_far.1, ...), custom_call_target="tpu_custom_call" | custom-call | tf_op jit(solution)/shard_map/halo/pallas_call | solution.py:461
  11.2 2.5 %windows.1 = bf16[4,9,640,128]{3,2,1,0:T(8,128)(2,1)S(1)} custom-call(s32[4,27]{1,0:T(4,128)} %owner_dir.1, s32[4,27]{1,0:T(4,128)} %owner_slot.1, f32[4,512,128]{2,1,0:T(8,128)S(1)} %get-tuple-element.14.split_grad, f32[6,3,32,128]{3,2,1,0:T(8,128)S(1)} %get-tuple-element.15.face_in, f32[12,3,8,128]{3,2,1,0:T(8,128)S(1)} %get-tuple-element.16.edge_in, ...), custom_call_target="tpu_custom_call" | custom-call | tf_op jit(solution)/shard_map/windows/pallas_call | solution.py:484
  13.7 0.0 copy-done
  13.7 0.0 copy-done.1
  13.7 31.0 %conv.1 = (f32[4,64,512]{2,1,0:T(8,128)S(1)}, f32[4,32,8,128]{3,2,1,0:T(8,128)S(1)}) custom-call(bf16[4,9,640,128]{3,2,1,0:T(8,128)(2,1)S(1)} %windows.1, f32[4,64,512]{2,1,0:T(8,128)S(1)} %copy-done.1, f32[4,512]{1,0:T(4,128)S(1)} %get-tuple-element.18.voxel_mask, f32[27,64,64]{2,1,0:T(8,128)S(1)} %copy-done, f32[8,128]{1,0:T(8,128)S(1)} %get-tuple-element.19.bias), custom_call_target="tpu_custom_call" | custom-call | tf_op jit(solution)/shard_map/conv/pallas_call | solution.py:501
  44.7 1.7 %finish.1 = (f32[4,64,512]{2,1,0:T(8,128)}, f32[27,64,64]{2,1,0:T(8,128)}, f32[1,64]{1,0:T(1,128)}) custom-call(f32[4,32,8,128]{3,2,1,0:T(8,128)S(1)} %get-tuple-element.20.full, f32[4,64,512]{2,1,0:T(8,128)S(1)} %get-tuple-element.21.result), custom_call_target="tpu_custom_call" | custom-call | tf_op jit(solution)/shard_map/finish/pallas_call | solution.py:523
Async XLA Ops:
  0.6 13.1 %copy-start = (f32[27,64,64]{2,1,0:T(8,128)S(1)}, f32[27,64,64]{2,1,0:T(8,128)}, u32[]{:S(2)}) copy-start(f32[27,64,64]{2,1,0:T(8,128)} %weights.1) | copy-start | bytes 1327108
  0.6 13.1 %copy-start.1 = (f32[4,64,512]{2,1,0:T(8,128)S(1)}, f32[4,64,512]{2,1,0:T(8,128)}, u32[]{:S(2)}) copy-start(f32[4,64,512]{2,1,0:T(8,128)} %features.1) | copy-start | bytes 1572868

commit v6 on v5

--- a/solution.py
+++ b/solution.py
@@ -491,7 +491,7 @@
         name="windows",
     )(in_hbm(owner_dir), in_hbm(owner_slot), split_grad, *landed)
     groups = stage_sizes(sizes)
-    chunks = min(4, max(1, 2 * channels // math.prod(groups)))
+    chunks = 1
     pair_tiles = channels // BS
     step = chunks * math.lcm(math.prod(groups), pair_tiles)
     tiles = -(-((taps + 1) // 2 * pair_tiles) // step) * step // chunks

time: 46.8 us -> 38.1 us (0.81)
  Pallas kernels: 45.8 us -> 37.1 us
    pallas_call x1, Pallas kernels: 31 us -> 22.4 us  [shards(): pl.pallas_call(functools.partial(conv_kernel, sizes, chunks), out_shape=[...]
where the time goes in v6:
time: 38.1 us; the launch traced here: 37.8 us
  Pallas kernels  37.1 us (97%)
  between operations  0.69 us (2%)
    pallas_call x1, Pallas kernels, shards(): pl.pallas_call(functools.partial(conv_kernel, sizes, chunks), out_shape=[...  22.4 us
    pallas_call x1, Pallas kernels, shards(): pl.pallas_call(functools.partial(halo_kernel, sizes), out_shape=[shaped((...  10.6 us
    pallas_call x1, Pallas kernels, shards(): pl.pallas_call(window_kernel, out_shape=shaped((blocks, 9, (BS + 2) * BS...  2.41 us
    pallas_call x1, Pallas kernels, shards(): pl.pallas_call(functools.partial(finish_kernel, scaling), out_shape=[shap...  1.74 us

profile of v6, /device:TPU:0, one launch (start us, length us, event | category | flops | bytes accessed | tf_op | source)
XLA Modules:
  0.0 37.8 jit_solution(6813109800146333779)
XLA Ops:
  0.6 0.0 copy-start
  0.6 0.0 copy-start.1
  0.7 10.6 %halo.1 = (f32[4,512,128]{2,1,0:T(8,128)S(1)}, f32[8,128]{1,0:T(8,128)S(1)}, f32[4,512]{1,0:T(4,128)S(1)}, f32[6,3,32,128]{3,2,1,0:T(8,128)S(1)}, f32[12,3,8,128...) custom-call(s32[3]{0:T(128)} %send_list.1, f32[4,64,512]{2,1,0:T(8,128)} %preact_far.1, f32[4,64,512]{2,1,0:T(8,128)} %cotangent_far.1, ...), custom_call_target="tpu_custom_call" | custom-call | tf_op jit(solution)/shard_map/halo/pallas_call | solution.py:461
  11.2 2.4 %windows.1 = bf16[4,9,640,128]{3,2,1,0:T(8,128)(2,1)S(1)} custom-call(s32[4,27]{1,0:T(4,128)} %owner_dir.1, s32[4,27]{1,0:T(4,128)} %owner_slot.1, f32[4,512,128]{2,1,0:T(8,128)S(1)} %get-tuple-element.14.split_grad, f32[6,3,32,128]{3,2,1,0:T(8,128)S(1)} %get-tuple-element.15.face_in, f32[12,3,8,128]{3,2,1,0:T(8,128)S(1)} %get-tuple-element.16.edge_in, ...), custom_call_target="tpu_custom_call" | custom-call | tf_op jit(solution)/shard_map/windows/pallas_call | solution.py:484
  13.6 0.0 copy-done
  13.6 0.0 copy-done.1
  13.7 22.4 %conv.1 = (f32[4,64,512]{2,1,0:T(8,128)S(1)}, f32[1,128,8,128]{3,2,1,0:T(8,128)S(1)}) custom-call(bf16[4,9,640,128]{3,2,1,0:T(8,128)(2,1)S(1)} %windows.1, f32[4,64,512]{2,1,0:T(8,128)S(1)} %copy-done.1, f32[4,512]{1,0:T(4,128)S(1)} %get-tuple-element.18.voxel_mask, f32[27,64,64]{2,1,0:T(8,128)S(1)} %copy-done, f32[8,128]{1,0:T(8,128)S(1)} %get-tuple-element.19.bias), custom_call_target="tpu_custom_call" | custom-call | tf_op jit(solution)/shard_map/conv/pallas_call | solution.py:501
  36.0 1.7 %finish.1 = (f32[4,64,512]{2,1,0:T(8,128)}, f32[27,64,64]{2,1,0:T(8,128)}, f32[1,64]{1,0:T(1,128)}) custom-call(f32[1,128,8,128]{3,2,1,0:T(8,128)S(1)} %get-tuple-element.20.full, f32[4,64,512]{2,1,0:T(8,128)S(1)} %get-tuple-element.21.result), custom_call_target="tpu_custom_call" | custom-call | tf_op jit(solution)/shard_map/finish/pallas_call | solution.py:523
Async XLA Ops:
  0.6 13.0 %copy-start = (f32[27,64,64]{2,1,0:T(8,128)S(1)}, f32[27,64,64]{2,1,0:T(8,128)}, u32[]{:S(2)}) copy-start(f32[27,64,64]{2,1,0:T(8,128)} %weights.1) | copy-start | bytes 1327108
  0.6 13.0 %copy-start.1 = (f32[4,64,512]{2,1,0:T(8,128)S(1)}, f32[4,64,512]{2,1,0:T(8,128)}, u32[]{:S(2)}) copy-start(f32[4,64,512]{2,1,0:T(8,128)} %features.1) | copy-start | bytes 1572868
